TPU v7x, 32 devices: a whole 2x2x4 slice. The times are simulated.
32 devices in a mesh: seq: 8 (over z, x), ch: 4 (over y, core).
Axes of the slice: x: 2, y: 2, z: 4, core: 2. Of those that a mesh axis runs over, the one named last changes fastest.
Arguments:
- tokens: float32 [8192, 1280], P('seq'), may hold values from -6 to 6
- cotangent: float32 [8192, 1280], P('seq', 'ch'), may hold values from -6 to 6
- lengths: int32 [16], replicated, may hold values from 30 to 1024, as said below
- valid_mask: int32 [8192], P('seq'), may hold values from 0 to 1, as said below
- weight_first: float32 [1280, 640], P(None, 'ch'), may hold values from -0.15625 to 0.15625
- weight_dilated: float32 [5, 640, 640], P(None, None, 'ch'), may hold values from -0.109375 to 0.109375
- weight_last: float32 [640, 1280], P('ch'), may hold values from -0.25 to 0.25
- momentum_first: float32 [1280, 640], P(None, 'ch'), may hold values from -320 to 320
- momentum_dilated: float32 [5, 640, 640], P(None, None, 'ch'), may hold values from -320 to 320
- momentum_last: float32 [640, 1280], P('ch'), may hold values from -320 to 320
- vector_params: float32 [7680], replicated, may hold values from -2 to 2
- vector_moment: float32 [7680], replicated, may hold values from -32 to 32
- vector_square: float32 [7680], replicated, may hold values from 2.94912 to 11.79648
Outputs:
- block_output: float32 [8192, 1280], P('seq', 'ch')
- tokens_grad: float32 [8192, 1280], P('seq', 'ch')
- first_weight: float32 [1280, 640], P(None, 'ch')
- dilated_weight: float32 [5, 640, 640], P(None, None, 'ch')
- last_weight: float32 [640, 1280], P('ch')
- first_momentum: float32 [1280, 640], P(None, 'ch')
- dilated_momentum: float32 [5, 640, 640], P(None, None, 'ch')
- last_momentum: float32 [640, 1280], P('ch')
- vector_first: float32 [7680], replicated
- vector_second: float32 [7680], replicated
- vector_values: float32 [7680], replicated
- root_means: float32 [2], replicated
Inputs may be any that keep to these rules, and one draw needn't show every extreme that they name: The lengths sum to 8192; the largest is exactly 1024. `valid_mask`: position 0 is valid.
All inputs are finite; a program needn't handle non-finite values.
Results may differ from a plain program's by a relative error of at most 0.0081.
Values may be sent and summed in bfloat16 or wider, within the bound.
No kernel may reach another device: no remote copies, remote signals or barrier semaphores. Data moves between devices by JAX's collectives and lax.ppermute only.
A program may use at most 256 MiB of HBM per device.

v0:
```python
import math

import jax
import jax.numpy as jnp
from jax import lax
from jax.sharding import PartitionSpec as P

D = 1280
INNER = 640
KERNEL_TAPS = 5
DILATION_SPAN = 128
STEP = 10


norm_eps = 1e-05
coef_first = 3.4445
coef_second = -4.775
coef_third = 2.0315
adam_rate = 0.4
adam_first = 0.9
adam_second = 0.999
adam_eps = 1e-08
decay_rate = 0.01
muon_rate = 0.1
muon_keep = 0.95
muon_scale = 0.2
highest = lax.Precision.HIGHEST
contract_rows = (((0,), (0,)), ((), ()))
contract_cols = (((1,), (1,)), ((), ()))


def padded(block, sides, width):
    for axis, dim in sides:
        count = lax.axis_size(axis)
        forward = [(i, i + 1) for i in range(count - 1)]
        backward = [(target, source) for source, target in forward]
        low = lax.ppermute(
            lax.slice_in_dim(block, block.shape[dim] - width, None, axis=dim), axis, forward
        )
        high = lax.ppermute(lax.slice_in_dim(block, 0, width, axis=dim), axis, backward)
        block = jnp.concatenate([low, block, high], axis=dim)
    return block


def shortened(shard):
    return jax.tree.map(lambda a: a.astype(jnp.bfloat16) if a.dtype == jnp.float32 else a, shard)


def smooth_gate(values):
    return jax.nn.gelu(values, approximate=False)


def segment_of(lengths, positions):
    bounds = jnp.cumsum(lengths)
    return jnp.sum((positions[:, None] >= bounds[None, :]).astype(jnp.int32), axis=1)


def forward_stats(values):
    totals = lax.psum((jnp.sum(values, axis=1), jnp.sum(values * values, axis=1)), "ch")
    center = totals[0][:, None] / INNER
    square = totals[1][:, None] / INNER - center * center
    return (center, lax.rsqrt(square + norm_eps))


def norm_backward(grad_active, normed, scale, gain):
    grad_normed = grad_active * gain
    totals = lax.psum((jnp.sum(grad_normed, axis=1), jnp.sum(grad_normed * normed, axis=1)), "ch")
    grad_values = scale * (
        grad_normed - totals[0][:, None] / INNER - normed * totals[1][:, None] / INNER
    )
    return (grad_values, jnp.sum(grad_active * normed, axis=0), jnp.sum(grad_active, axis=0))


def orthogonal(matrix):
    rows_count, cols_count = matrix.shape
    work = matrix / (jnp.sqrt(jnp.sum(matrix * matrix)) + 1e-07)
    for sweep_index in range(5):
        if rows_count >= cols_count:
            gram = jnp.dot(work.T, work, precision=highest, preferred_element_type=jnp.float32)
            poly = coef_second * gram + coef_third * jnp.dot(
                gram, gram, precision=highest, preferred_element_type=jnp.float32
            )
            work = coef_first * work + jnp.dot(
                work, poly, precision=highest, preferred_element_type=jnp.float32
            )
        else:
            gram = jnp.dot(work, work.T, precision=highest, preferred_element_type=jnp.float32)
            poly = coef_second * gram + coef_third * jnp.dot(
                gram, gram, precision=highest, preferred_element_type=jnp.float32
            )
            work = coef_first * work + jnp.dot(
                poly, work, precision=highest, preferred_element_type=jnp.float32
            )
    return work * (muon_scale * math.sqrt(max(rows_count, cols_count)))


def body(
    tokens,
    cotangent,
    lengths,
    valid_mask,
    weight_first,
    weight_dilated,
    weight_last,
    momentum_first,
    momentum_dilated,
    momentum_last,
    vector_params,
    vector_moment,
    vector_square,
):
    groups = lax.axis_size("ch")
    member = lax.axis_index("ch")
    seq_count = lax.axis_size("seq")
    local_rows = tokens.shape[0]
    inner_local = weight_first.shape[1]
    model_local = D // groups
    neighbour_rows = KERNEL_TAPS // 2 * DILATION_SPAN
    valid = valid_mask.astype(jnp.float32)
    positions = (
        lax.axis_index("seq") * local_rows
        + jnp.arange(local_rows + 2 * neighbour_rows, dtype=jnp.int32)
        - neighbour_rows
    )
    segment = segment_of(lengths, positions)
    centre = segment[neighbour_rows : neighbour_rows + local_rows]
    masks = []
    for kernel_tap_index in range(KERNEL_TAPS):
        tap_offset = neighbour_rows + (kernel_tap_index - KERNEL_TAPS // 2) * DILATION_SPAN
        masks.append((segment[tap_offset : tap_offset + local_rows] == centre).astype(jnp.float32))

    def own_piece(base, count):
        return lax.dynamic_slice_in_dim(vector_params, base + member * count, count, 0)

    gain_one = vector_params[0:D]
    shift_one = vector_params[D : 2 * D]
    bias_one = own_piece(2 * D, inner_local)
    gain_two = own_piece(2 * D + INNER, inner_local)
    shift_two = own_piece(2 * D + 2 * INNER, inner_local)
    bias_two = own_piece(2 * D + 3 * INNER, inner_local)
    gain_three = own_piece(2 * D + 4 * INNER, inner_local)
    shift_three = own_piece(2 * D + 5 * INNER, inner_local)
    bias_three = own_piece(2 * D + 6 * INNER, model_local)
    center_one = jnp.mean(tokens, axis=1, keepdims=True)
    square_one = jnp.mean(tokens * tokens, axis=1, keepdims=True) - center_one * center_one
    scale_one = lax.rsqrt(square_one + norm_eps)
    normed_one = (tokens - center_one) * scale_one
    active_one = normed_one * gain_one + shift_one
    hidden_one = smooth_gate(active_one).astype(jnp.bfloat16)
    first_low = weight_first.astype(jnp.bfloat16)
    inner_one = jnp.dot(hidden_one, first_low, preferred_element_type=jnp.float32) + bias_one
    center_two, scale_two = forward_stats(inner_one)
    normed_two = (inner_one - center_two) * scale_two
    active_two = normed_two * gain_two + shift_two
    gated_two, slope_two = jax.vjp(smooth_gate, active_two)
    hidden_two = (gated_two * valid[:, None]).astype(jnp.bfloat16)
    rimmed = padded(hidden_two, (("seq", 0),), neighbour_rows)
    channels = lax.all_gather(rimmed, "ch", axis=1, tiled=True)
    kernel = weight_dilated.astype(jnp.bfloat16)
    summed = jnp.zeros((local_rows, inner_local), jnp.float32)
    for kernel_tap_index in range(KERNEL_TAPS):
        tap_offset = neighbour_rows + (kernel_tap_index - KERNEL_TAPS // 2) * DILATION_SPAN
        product = jnp.dot(
            channels[tap_offset : tap_offset + local_rows],
            kernel[kernel_tap_index],
            preferred_element_type=jnp.float32,
        )
        summed = summed + masks[kernel_tap_index][:, None] * product
    inner_two = summed + bias_two
    center_three, scale_three = forward_stats(inner_two)
    normed_three = (inner_two - center_three) * scale_three
    active_three = normed_three * gain_three + shift_three
    gated_three, slope_three = jax.vjp(smooth_gate, active_three)
    hidden_three = gated_three.astype(jnp.bfloat16)
    last_low = weight_last.astype(jnp.bfloat16)
    partial_out = jnp.dot(hidden_three, last_low, preferred_element_type=jnp.float32)
    branch = lax.psum_scatter(partial_out, "ch", scatter_dimension=1, tiled=True) + bias_three
    own_tokens = lax.dynamic_slice_in_dim(tokens, member * model_local, model_local, 1)
    block_output = own_tokens + branch
    grad_bias_three = jnp.sum(cotangent, axis=0)
    grad_rows = lax.all_gather(cotangent.astype(jnp.bfloat16), "ch", axis=1, tiled=True)
    grad_last = lax.dot_general(
        hidden_three, grad_rows, contract_rows, preferred_element_type=jnp.float32
    )
    grad_hidden_three = lax.dot_general(
        grad_rows, last_low, contract_cols, preferred_element_type=jnp.float32
    )
    grad_active_three = slope_three(grad_hidden_three)[0]
    grad_inner_two, grad_gain_three, grad_shift_three = norm_backward(
        grad_active_three, normed_three, scale_three, gain_three
    )
    grad_bias_two = jnp.sum(grad_inner_two, axis=0)
    inner_two_low = grad_inner_two.astype(jnp.bfloat16)
    grad_rimmed = padded(inner_two_low, (("seq", 0),), neighbour_rows)
    feedback = jnp.zeros((local_rows, INNER), jnp.float32)
    kernel_grads = []
    for kernel_tap_index in range(KERNEL_TAPS):
        moved_rows = (kernel_tap_index - KERNEL_TAPS // 2) * DILATION_SPAN
        begin = neighbour_rows - moved_rows
        incoming = lax.dot_general(
            grad_rimmed[begin : begin + local_rows],
            kernel[kernel_tap_index],
            contract_cols,
            preferred_element_type=jnp.float32,
        )
        feedback = feedback + masks[KERNEL_TAPS - 1 - kernel_tap_index][:, None] * incoming
        masked_grad = inner_two_low * masks[kernel_tap_index].astype(jnp.bfloat16)[:, None]
        source_rows = channels[
            neighbour_rows + moved_rows : neighbour_rows + moved_rows + local_rows
        ]
        kernel_grads.append(
            lax.dot_general(
                source_rows, masked_grad, contract_rows, preferred_element_type=jnp.float32
            )
        )
    grad_dilated = jnp.stack(kernel_grads)
    feedback_own = lax.psum_scatter(feedback, "ch", scatter_dimension=1, tiled=True)
    grad_active_two = slope_two(feedback_own * valid[:, None])[0]
    grad_inner_one, grad_gain_two, grad_shift_two = norm_backward(
        grad_active_two, normed_two, scale_two, gain_two
    )
    grad_bias_one = jnp.sum(grad_inner_one, axis=0)
    inner_one_low = grad_inner_one.astype(jnp.bfloat16)
    grad_first = lax.dot_general(
        hidden_one, inner_one_low, contract_rows, preferred_element_type=jnp.float32
    )
    partial_input = lax.dot_general(
        inner_one_low, first_low, contract_cols, preferred_element_type=jnp.float32
    )
    total_input = lax.psum(partial_input, "ch")
    unused, slope_one = jax.vjp(smooth_gate, active_one)
    grad_active_one = slope_one(total_input)[0]
    grad_normed_one = grad_active_one * gain_one
    mean_grad = jnp.mean(grad_normed_one, axis=1, keepdims=True)
    mean_cross = jnp.mean(grad_normed_one * normed_one, axis=1, keepdims=True)
    grad_full = scale_one * (grad_normed_one - mean_grad - normed_one * mean_cross)
    grad_own = lax.dynamic_slice_in_dim(grad_full, member * model_local, model_local, 1)
    grad_gain_one = lax.dynamic_slice_in_dim(
        jnp.sum(grad_active_one * normed_one, axis=0), member * model_local, model_local, 0
    )
    grad_shift_one = lax.dynamic_slice_in_dim(
        jnp.sum(grad_active_one, axis=0), member * model_local, model_local, 0
    )
    tokens_grad = cotangent + grad_own

    def put_piece(vector, values, base):
        return lax.dynamic_update_slice_in_dim(vector, values, base + member * values.shape[0], 0)

    grad_vector = jnp.zeros((3 * D + 6 * INNER,), jnp.float32)
    grad_vector = put_piece(grad_vector, grad_gain_one, 0)
    grad_vector = put_piece(grad_vector, grad_shift_one, D)
    grad_vector = put_piece(grad_vector, grad_bias_one, 2 * D)
    grad_vector = put_piece(grad_vector, grad_gain_two, 2 * D + INNER)
    grad_vector = put_piece(grad_vector, grad_shift_two, 2 * D + 2 * INNER)
    grad_vector = put_piece(grad_vector, grad_bias_two, 2 * D + 3 * INNER)
    grad_vector = put_piece(grad_vector, grad_gain_three, 2 * D + 4 * INNER)
    grad_vector = put_piece(grad_vector, grad_shift_three, 2 * D + 5 * INNER)
    grad_vector = put_piece(grad_vector, grad_bias_three, 2 * D + 6 * INNER)
    local_stats = jnp.stack(
        [
            jnp.sum(valid[:, None] * block_output * block_output),
            jnp.sum(valid[:, None] * branch * branch),
            jnp.sum(valid) / groups,
        ]
    )
    grad_vector, total_stats = lax.psum((grad_vector, local_stats), ("seq", "ch"))
    grad_first, grad_dilated, grad_last = lax.psum((grad_first, grad_dilated, grad_last), "seq")
    keep_weight = 1.0 - muon_rate * decay_rate
    first_momentum = muon_keep * momentum_first + grad_first
    dilated_momentum = muon_keep * momentum_dilated + grad_dilated
    last_momentum = muon_keep * momentum_last + grad_last
    whole_first, whole_dilated, whole_last = (
        lax.all_gather(first_momentum, "ch", axis=1, tiled=True),
        lax.all_gather(dilated_momentum, "ch", axis=2, tiled=True),
        lax.all_gather(last_momentum, "ch", axis=0, tiled=True),
    )
    pack_size = D * inner_local
    tap_size = INNER * inner_local

    def pad_flat(values):
        flat = values.reshape(-1)
        return jnp.pad(flat, (0, pack_size - flat.shape[0]))

    def run_first():
        return pad_flat(
            lax.dynamic_slice_in_dim(orthogonal(whole_first), member * inner_local, inner_local, 1)
        )

    def make_tap(kernel_tap_index):

        def run_tap():
            return pad_flat(
                lax.dynamic_slice_in_dim(
                    orthogonal(whole_dilated[kernel_tap_index]),
                    member * inner_local,
                    inner_local,
                    1,
                )
            )

        return run_tap

    def run_last():
        return pad_flat(
            lax.dynamic_slice_in_dim(orthogonal(whole_last), member * inner_local, inner_local, 0)
        )

    def run_none():
        return jnp.zeros((pack_size,), jnp.float32)

    branches = (
        [run_first]
        + [make_tap(kernel_tap_index) for kernel_tap_index in range(KERNEL_TAPS)]
        + [run_last, run_none]
    )
    owner = jnp.minimum(seq_count - 1 - lax.axis_index("seq"), KERNEL_TAPS + 2)
    packed = lax.switch(owner, branches)
    all_steps = lax.all_gather(shortened(packed[None, :]), "seq", axis=0, tiled=True)
    step_first = all_steps[seq_count - 1].reshape(D, inner_local)
    step_dilated = jnp.stack(
        [
            all_steps[seq_count - 2 - kernel_tap_index][:tap_size].reshape(INNER, inner_local)
            for kernel_tap_index in range(KERNEL_TAPS)
        ]
    )
    step_last = all_steps[seq_count - 2 - KERNEL_TAPS].reshape(inner_local, D)
    first_weight = weight_first * keep_weight - muon_rate * step_first
    dilated_weight = weight_dilated * keep_weight - muon_rate * step_dilated
    last_weight = weight_last * keep_weight - muon_rate * step_last
    vector_first = adam_first * vector_moment + (1.0 - adam_first) * grad_vector
    vector_second = adam_second * vector_square + (1.0 - adam_second) * grad_vector * grad_vector
    corrected_first = vector_first / (1.0 - adam_first**STEP)
    corrected_second = vector_second / (1.0 - adam_second**STEP)
    vector_values = vector_params - adam_rate * (
        corrected_first / (jnp.sqrt(corrected_second) + adam_eps) + decay_rate * vector_params
    )
    root_means = jnp.stack(
        [
            jnp.sqrt(total_stats[0] / (total_stats[2] * D)),
            jnp.sqrt(total_stats[1] / (total_stats[2] * D)),
        ]
    )
    return (
        block_output,
        tokens_grad,
        first_weight,
        dilated_weight,
        last_weight,
        first_momentum,
        dilated_momentum,
        last_momentum,
        vector_first,
        vector_second,
        vector_values,
        root_means,
    )


def solution(mesh):
    placed = (
        P("seq", None),
        P("seq", "ch"),
        P(),
        P("seq"),
        P(None, "ch"),
        P(None, None, "ch"),
        P("ch", None),
        P(None, "ch"),
        P(None, None, "ch"),
        P("ch", None),
        P(),
        P(),
        P(),
    )
    return jax.shard_map(
        body,
        mesh=mesh,
        in_specs=placed,
        out_specs=(
            P("seq", "ch"),
            P("seq", "ch"),
            P(None, "ch"),
            P(None, None, "ch"),
            P("ch", None),
            P(None, "ch"),
            P(None, None, "ch"),
            P("ch", None),
            P(),
            P(),
            P(),
            P(),
        ),
        check_vma=False,
    )
```

profile of v0, /device:TPU:0, one launch (start us, length us, event | category | flops | bytes accessed | tf_op | source)
XLA Modules:
  0.0 756.9 jit_solution(13509502838518582919)
XLA Ops:
  8.7 3.2 fusion.437
  11.9 15.6 %multiply_convert_fusion = (bf16[1024,1280]{1,0:T(8,128)(2,1)S(1)}, f32[1024,1280]{1,0:T(8,128)}, f32[1024,1280]{1,0:T(8,128)}) fusion(f32[1280]{0:T(1024)S(1)} %get-tuple-element.188, f32[1280]{0:T(1024)S(1)} %get-tuple-element.187, f32[1024]{0:T(1024)S(1)} %get-tuple-element.200, f32[1024,1280]{1,0:T(8,128)} %param.21, f32[1024]{0:T(1024)S(1)} %get-tuple-element.199), kind=kLoop, calls=%fused_computation.362 | loop fusion | flops 90439680 | bytes 18368512 | tf_op jit(solution)/shard_map/convert_element_type | solution.py:149
  28.4 1.8 fusion.439
  30.3 8.5 %all-reduce.10 = (f32[1024]{0:T(1024)S(1)}, f32[1024]{0:T(1024)S(1)}) all-reduce(f32[1024]{0:T(1024)S(1)} %get-tuple-element.134, f32[1024]{0:T(1024)S(1)} %get-tuple-element.133), channel_id=1, replica_groups=mesh['seq'=8,'ch'=4] {'ch'}, use_global_device_ids=true, to_apply=%region_7.8 | all-reduce | flops 2048 | bytes 16384 | tf_op jit(solution)/shard_map/psum | solution.py:59
  38.8 3.6 multiply_convert_fusion.2
  43.7 4.6 collective-permute-start
  48.7 1.6 collective-permute-done
  51.2 3.3 fusion.452
  54.8 2.6 convert_element_type.98
  57.6 17.6 %all-gather.8.cloned.1.call-done = bf16[1536,640]{0,1:T(8,128)(2,1)} async-done(((bf16[1536,160]{0,1:T(8,128)(2,1)}), bf16[1536,640]{0,1:T(8,128)(2,1)}) %all-gather.8.cloned.1.call-update) | async-done | bytes 1966096 | tf_op jit(solution)/shard_map/all_gather | solution.py:158
  75.1 2.0 convolution_multiply_fusion.3
  80.8 6.0 all-reduce.9
  86.8 16.1 %all-gather.10.cloned.1.call-done = bf16[1024,1280]{0,1:T(8,128)(2,1)} async-done(((bf16[1024,320]{0,1:T(8,128)(2,1)}), bf16[1024,1280]{0,1:T(8,128)(2,1)}) %all-gather.10.cloned.1.call-update) | async-done | bytes 2621456 | tf_op jit(solution)/shard_map/all_gather | solution.py:181
  102.9 5.1 multiply_reduce_fusion.17
  108.0 6.0 all-reduce.8
  114.0 3.9 multiply_reduce_fusion.10
  118.0 1.5 collective-permute-start.2
  120.0 4.5 collective-permute-start.3
  127.2 2.6 multiply_add_fusion.17
  129.9 2.0 fusion.370
  135.8 1.9 fusion.521
  137.8 29.8 %reduce-scatter.5.cloned.1.call-done = f32[1024,160]{0,1:T(8,128)} async-done(((f32[1024,640]{0,1:T(8,128)}), f32[1024,160]{0,1:T(8,128)}) %reduce-scatter.5.cloned.1.call-update) | async-done | bytes 655376 | tf_op jit(solution)/shard_map/reduce_scatter | solution.py:217
  167.5 3.5 multiply_reduce_fusion.11
  171.0 5.8 all-reduce.7
  176.9 2.2 fusion.441
  179.8 1.5 fusion.422
  181.4 145.3 %all-reduce.16.cloned.1.call-done = (f32[1280,160]{0,1:T(8,128)}, f32[5,640,160]{1,2,0:T(8,128)}, f32[160,1280]{1,0:T(8,128)}) async-done(((f32[1280,160]{0,1:T(8,128)}, f32[5,640,160]{1,2,0:T(8,128)}, f32[160,1280]{1,0:T(8,128)}), (f32[1280,160]{0,1:T(8,128)}, f32[5,640,160]{1,2,0:T(8,128)}, f32[160,1280]{1,0:T(8,128)})) %all-reduce.16.cloned.1.call-update) | async-done | bytes 3686416 | tf_op jit(solution)/shard_map/psum | solution.py:267
  326.7 2.2 multiply_add_fusion.20
  329.0 2.3 multiply_add_fusion.19
  331.4 3.1 multiply_add_fusion.18
  335.8 3.2 fusion.414
  340.2 3.3 fusion.410
  343.6 13.8 %all-gather.12.cloned.1.call-done = f32[1280,640]{0,1:T(8,128)} async-done(((f32[1280,160]{0,1:T(8,128)}), f32[1280,640]{0,1:T(8,128)}) %all-gather.12.cloned.1.call-update) | async-done | bytes 3276816 | tf_op jit(solution)/shard_map/all_gather | solution.py:273
  357.4 31.4 %all-gather.16.cloned.1.call-done = f32[640,1280]{1,0:T(8,128)} async-done(((f32[160,1280]{1,0:T(8,128)}), f32[640,1280]{1,0:T(8,128)}) %all-gather.16.cloned.1.call-update) | async-done | bytes 3276816 | tf_op jit(solution)/shard_map/all_gather | solution.py:275
  388.7 59.4 %all-gather.14.cloned.1.call-done = f32[5,640,640]{1,2,0:T(8,128)} async-done(((f32[5,640,160]{1,2,0:T(8,128)}), f32[5,640,640]{1,2,0:T(8,128)}) %all-gather.14.cloned.1.call-update) | async-done | bytes 8192016 | tf_op jit(solution)/shard_map/all_gather | solution.py:274
  448.2 41.7 %conditional.1 = (bf16[204800]{0:T(1024)(128)(2,1)S(1)}) conditional(s32[]{:T(128)} %clamp.3, (f32[1280,640]{0,1:T(8,128)}, s32[]{:T(128)}) %tuple.32, (f32[5,640,640]{1,2,0:T(8,128)}, s32[]{:T(128)}) %tuple.33, (f32[5,640,640]{1,2,0:T(8,128)}, s32[]{:T(128)}) %tuple.33, (f32[5,640,640]{1,2,0:T(8,128)}, ...), branch_computations={%region_28.30_spmd, %region_30.32_spmd, %region_32.34_spmd, %regio... | conditional | flops 78660812800 | bytes 110182520 | solution.py:317
  490.6 3.1 copy.65
  493.7 1.5 copy.66
  495.2 3.2 copy.67
  498.5 3.2 constant_dynamic-slice_fusion
  501.7 3.0 copy.71
  505.9 47.3 %all-reduce.14.cloned.1.call-done = f32[1024,1280]{1,0:T(8,128)} async-done(((f32[1024,1280]{1,0:T(8,128)}), f32[1024,1280]{1,0:T(8,128)}) %all-reduce.14.cloned.1.call-update) | async-done | bytes 5242896 | tf_op jit(solution)/shard_map/psum | solution.py:230
  553.2 7.7 %fusion.436 = (f32[1280]{0:T(1024)S(1)}, f32[1280]{0:T(1024)S(1)}, f32[1024]{0:T(1024)S(1)}, f32[1024]{0:T(1024)S(1)}, f32[1024,1280]{1,0:T(8,128)S(1)}) fusion(f32[1024,1280]{1,0:T(8,128)} %get-tuple-element.170, f32[1280]{0:T(1024)S(1)} %copy-done.24, f32[1024,1280]{1,0:T(8,128)} %all-reduce.14.cloned.1.call-done, f32[1024,1280]{1,0:T(8,128)} %get-tuple-element.169, ...), kind=kLoop, calls=%fused_computation.563 | loop fusion | flops 28831232 | bytes 21000192 | tf_op jit(solution)/shard_map/reduce_sum | solution.py:242
  560.9 4.7 fusion.359
  565.7 3.1 copy.68
  570.9 36.6 %reduce-scatter.3.cloned.1.call-done = f32[1024,320]{0,1:T(8,128)} async-done(((f32[1024,1280]{0,1:T(8,128)}), f32[1024,320]{0,1:T(8,128)}) %reduce-scatter.3.cloned.1.call-update) | async-done | bytes 1310736 | tf_op jit(solution)/shard_map/reduce_scatter | solution.py:177
  607.5 3.6 fusion.360
  612.5 79.9 %all-reduce.5 = (f32[7680]{0:T(1024)S(1)}, f32[3]{0:T(128)S(1)}) all-reduce(f32[7680]{0:T(1024)S(1)} %dynamic_update_slice.35, f32[3]{0:T(128)S(1)} %pad_maximum_fusion.5), channel_id=1, replica_groups=mesh['seq'=8,'ch'=4] {'seq','ch'}, use_global_device_ids=true, to_apply=%region_52.53 | all-reduce | flops 7683 | bytes 61464 | tf_op jit(solution)/shard_map/psum | solution.py:266
  696.3 2.4 fusion.393
  698.7 2.8 reshape.194
  701.4 2.9 multiply_subtract_fusion
  704.4 2.6 copy.69
  706.9 5.0 reshape.196
  712.0 11.0 %slice_reduce_fusion = (bf16[102400]{0:T(1024)(128)(2,1)S(1)}, bf16[102400]{0:T(1024)(128)(2,1)}, bf16[102400]{0:T(1024)(128)(2,1)}, bf16[102400]{0:T(1024)(128)(2,1)}, bf16[102400]{0:T(1024)(128)(2,1)}) fusion(bf16[8,204800]{1,0:T(8,128)(2,1)} %reshape.196), kind=kLoop, calls=%fused_computation.478 | loop fusion | bytes 2048000 | tf_op jit(solution)/shard_map/slice | solution.py:322
  723.0 2.0 stack_reshape.15
  725.0 1.7 constant_dynamic-update-slice_fusion.4
  726.7 2.0 stack_reshape.16
  728.7 2.0 stack_reshape.17
  730.6 2.0 stack_reshape.18
  733.7 1.8 constant_dynamic-update-slice_fusion.3
  735.5 1.7 constant_dynamic-update-slice_fusion.2
  737.2 1.7 constant_dynamic-update-slice_fusion.1
  739.6 3.5 convert_subtract_fusion
  743.2 4.4 copy.70
  (156 shorter events, 30.5 us)
Async XLA Ops:
  7.2 68.0 %all-gather.8.cloned.1.call-start = ((), (), s32[]{:S(2)}) async-start(), calls=%async_computation.2 | async-start | bytes 2457600 | tf_op jit(solution)/shard_map/all_gather | solution.py:158
  7.9 159.6 %copy-start.27 = (f32[1024]{0:T(1024)}, f32[1024]{0:T(1024)S(1)}, u32[]{:S(2)}) copy-start(f32[1024]{0:T(1024)S(1)} %convert_element_type.96) | copy-start | bytes 12292
  8.7 3.2 copy-start.23
  8.7 3.2 copy-start.25
  11.9 15.6 %copy-start.29 = (f32[1024]{0:T(1024)}, f32[1024]{0:T(1024)S(1)}, u32[]{:S(2)}) copy-start(f32[1024]{0:T(1024)S(1)} %get-tuple-element.200) | copy-start | bytes 12292
  11.9 16.5 %copy-start.7 = (f32[1280,160]{0,1:T(8,128)S(1)}, f32[1280,160]{0,1:T(8,128)}, u32[]{:S(2)}) copy-start(f32[1280,160]{0,1:T(8,128)} %param.25) | copy-start | bytes 2457604
  42.4 6.3 collective-permute-start.1
  43.7 6.6 collective-permute-start
  51.1 3.5 copy-start.41
  51.1 51.7 %all-gather.10.cloned.1.call-start = ((), (), s32[]{:S(2)}) async-start(), calls=%async_computation.4 | async-start | bytes 3276800 | tf_op jit(solution)/shard_map/all_gather | solution.py:181
  54.5 113.0 %reduce-scatter.5.cloned.1.call-start = ((), (), s32[]{:S(2)}) async-start(), calls=%async_computation.5 | async-start | bytes 3276800 | tf_op jit(solution)/shard_map/reduce_scatter | solution.py:217
  75.1 2.0 copy-start
  77.1 1.5 copy-start.2
  114.0 5.5 copy-start.3
  118.0 6.6 collective-permute-start.2
  120.0 6.6 collective-permute-start.3
  129.8 196.9 %all-reduce.16.cloned.1.call-start = ((), (), s32[]{:S(2)}) async-start(), calls=%async_computation.11 | async-start | bytes 7372800 | tf_op jit(solution)/shard_map/psum | solution.py:267
  129.9 2.0 copy-start.1
  133.6 2.2 copy-start.15
  134.2 1.3 copy-start.17
  179.1 0.7 copy-start.13
  181.3 145.4 %copy-start.20 = (f32[1280,160]{0,1:T(8,128)S(1)}, f32[1280,160]{0,1:T(8,128)}, u32[]{:S(2)}) copy-start(f32[1280,160]{0,1:T(8,128)} %param.28) | copy-start | bytes 2457604
  181.3 176.0 %all-gather.12.cloned.1.call-start = ((), (), s32[]{:S(2)}) async-start(), calls=%async_computation.7 | async-start | bytes 4096000 | tf_op jit(solution)/shard_map/all_gather | solution.py:273
  326.7 2.3 copy-start.21
  329.0 59.8 %all-gather.16.cloned.1.call-start = ((), (), s32[]{:S(2)}) async-start(), calls=%async_computation.9 | async-start | bytes 4096000 | tf_op jit(solution)/shard_map/all_gather | solution.py:275
  329.0 2.4 copy-start.16
  331.3 116.8 %all-gather.14.cloned.1.call-start = ((), (), s32[]{:S(2)}) async-start(), calls=%async_computation.8 | async-start | bytes 10240000 | tf_op jit(solution)/shard_map/all_gather | solution.py:274
  334.5 1.2 copy-start.8
  334.5 1.3 copy-start.14
  334.5 218.7 %all-reduce.14.cloned.1.call-start = ((), (), s32[]{:S(2)}) async-start(), calls=%async_computation.6 | async-start | bytes 10485760 | tf_op jit(solution)/shard_map/psum | solution.py:230
  339.0 1.1 copy-start.5
  339.0 268.5 %reduce-scatter.3.cloned.1.call-start = ((), (), s32[]{:S(2)}) async-start(), calls=%async_computation.3 | async-start | bytes 6553600 | tf_op jit(solution)/shard_map/reduce_scatter | solution.py:177
  343.5 352.8 %all-gather.18.cloned.1.call-start = ((), (), s32[]{:S(2)}) async-start(), calls=%async_computation.10 | async-start | bytes 3686400 | tf_op jit(solution)/shard_map/all_gather | solution.py:318
  489.8 0.8 copy-start.18
  490.6 3.1 copy-start.9
  495.2 3.2 copy-start.22
  501.7 3.0 copy-start.33
  501.7 51.5 %copy-start.24 = (f32[1280]{0:T(1024)S(1)}, f32[1280]{0:T(1024)}, u32[]{:S(2)}) copy-start(f32[1280]{0:T(1024)} %copy-done.23) | copy-start | bytes 15364
  501.7 51.5 %copy-start.26 = (f32[1280]{0:T(1024)S(1)}, f32[1280]{0:T(1024)}, u32[]{:S(2)}) copy-start(f32[1280]{0:T(1024)} %copy-done.25) | copy-start | bytes 15364
  553.2 7.7 %copy-start.4 = (f32[1024,320]{1,0:T(8,128)S(1)}, f32[1024,320]{1,0:T(8,128)}, u32[]{:S(2)}) copy-start(f32[1024,320]{1,0:T(8,128)} %copy.65) | copy-start | bytes 3932164
  553.2 7.7 %copy-start.30 = (f32[1024]{0:T(1024)S(1)}, f32[1024]{0:T(1024)}, u32[]{:S(2)}) copy-start(f32[1024]{0:T(1024)} %copy-done.29) | copy-start | bytes 12292
  565.6 3.5 copy-start.40
  565.6 3.7 copy-start.39
  565.6 4.0 copy-start.38
  565.6 4.2 copy-start.37
  565.6 4.5 copy-start.36
  565.6 4.7 copy-start.35
  565.7 5.0 copy-start.34
  565.7 41.8 %copy-start.28 = (f32[1024]{0:T(1024)S(1)}, f32[1024]{0:T(1024)}, u32[]{:S(2)}) copy-start(f32[1024]{0:T(1024)} %copy-done.27) | copy-start | bytes 12292
  570.9 124.7 %copy-start.31 = (f32[7680]{0:T(1024)S(1)}, f32[7680]{0:T(1024)}, u32[]{:S(2)}) copy-start(f32[7680]{0:T(1024)} %param.33) | copy-start | bytes 92164
  570.9 124.7 %copy-start.32 = (f32[7680]{0:T(1024)S(1)}, f32[7680]{0:T(1024)}, u32[]{:S(2)}) copy-start(f32[7680]{0:T(1024)} %param.32) | copy-start | bytes 92164
  733.7 5.2 copy-start.19
  743.2 4.4 copy-start.10
  747.6 1.1 copy-start.6
Sparse Core Ops, SparseCore 0:
  51.2 23.8 all-gather.7
  77.3 25.5 all-gather.9
  129.9 37.5 reduce-scatter.4
  181.4 145.2 all-reduce.15
  329.1 28.2 all-gather.11
  359.4 29.2 all-gather.15
  390.9 57.1 all-gather.13
  450.6 102.5 all-reduce.13
  555.9 51.5 reduce-scatter.2
  610.1 68.5 all-gather.17
where the time goes:
time: 767 us; the launch traced here: 757 us
  waiting for transfers between devices  400 us (52%)
  blocking collectives  106 us (14%)
  other arithmetic  76.3 us (10%)
  local copies, waits for them, and re-layouts  70.9 us (9%)
  loops' own time  41.6 us (5%)
  matrix products  31.6 us (4%)
  between operations  17.7 us (2%)
  starting transfers between devices  12.3 us (2%)
    psum x1, waiting for transfers between devices, body(): lax.psum((grad_first, grad_dilated, grad_last), 'seq')  145 us
    psum x1, blocking collectives, body(): lax.psum((grad_vector, local_stats), ('seq', 'ch'))  79.9 us
    all_gather x1, waiting for transfers between devices, body(): lax.all_gather(dilated_momentum, 'ch', axis=2, tiled=True)  59.4 us
    psum x1, waiting for transfers between devices, body(): total_input = lax.psum(partial_input, 'ch')  47.3 us
    another operation x1, loops' own time, body(): packed = lax.switch(owner, branches)  41.6 us
    reduce_scatter x1, waiting for transfers between devices, body(): lax.psum_scatter(partial_out, 'ch', scatter_dimension=1, tiled=True)  36.6 us
    unnamed x91, local copies, waits for them, and re-layouts  34.3 us
    all_gather x1, waiting for transfers between devices, body(): lax.all_gather(last_momentum, 'ch', axis=0, tiled=True)  31.4 us
  transfers between devices with their start and end apart: 14, of which 12 were waited for; matrix products, arithmetic and copies ran while one was open for 9% of the time, Pallas kernels for 0%

commit v1 on v0

v1 whole, which is shorter than its diff:
```python
import functools
import math

import jax
import jax.numpy as jnp
from jax import lax
from jax.experimental import pallas as pl
from jax.experimental.pallas import tpu as pltpu
from jax.sharding import PartitionSpec as P

D = 1280
INNER = 640
KERNEL_TAPS = 5
DILATION_SPAN = 128
STEP = 10

norm_eps = 1e-05
coef_first = 3.4445
coef_second = -4.775
coef_third = 2.0315
adam_rate = 0.4
adam_first = 0.9
adam_second = 0.999
adam_eps = 1e-08
decay_rate = 0.01
muon_rate = 0.1
muon_keep = 0.95
muon_scale = 0.2
REACH = KERNEL_TAPS // 2 * DILATION_SPAN
VECTOR = 3 * D + 6 * INNER
HALF_D = D // 2
MIB = 1024 * 1024

f32 = jnp.float32
bf16 = jnp.bfloat16
NN = (((1,), (0,)), ((), ()))
NT = (((1,), (1,)), ((), ()))
TN = (((0,), (0,)), ((), ()))


def mul(a, b, dims):
    return lax.dot_general(a, b, dims, preferred_element_type=f32)


def erf_parts(v):
    a = jnp.abs(v) * math.sqrt(0.5)
    t = pl.reciprocal(1.0 + 0.3275911 * a)
    e = jnp.exp(-a * a)
    p = t * (0.254829592 + t * (-0.284496736 + t * (1.421413741 + t * (-1.453152027 + t * 1.061405429))))
    tail = 0.5 * p * e
    return jnp.where(v >= 0, 1.0 - tail, tail), e


def gelu_pair(v):
    cdf, e = erf_parts(v)
    return v * cdf, cdf + v * e * (1.0 / math.sqrt(2.0 * math.pi))


VMEM = pl.BlockSpec(memory_space=pltpu.VMEM)
SMEM = pl.BlockSpec(memory_space=pltpu.SMEM)


def call(kernel, outs, scalars, arrays, scratch=(), limit=24, flops=10**8):
    shapes = [jax.ShapeDtypeStruct(shape, dtype) for shape, dtype in outs]
    size = sum(math.prod(shape) * jnp.dtype(dtype).itemsize for shape, dtype in outs)
    size += sum(a.size * a.dtype.itemsize for a in arrays)
    return pl.pallas_call(
        kernel,
        out_shape=shapes,
        in_specs=[SMEM] * len(scalars) + [VMEM] * len(arrays),
        out_specs=[VMEM] * len(outs),
        scratch_shapes=[pltpu.VMEM(shape, dtype) for shape, dtype in scratch],
        compiler_params=pltpu.CompilerParams(vmem_limit_bytes=limit * MIB),
        cost_estimate=pl.CostEstimate(flops=flops, bytes_accessed=size, transcendentals=0),
    )(*scalars, *arrays)


def chunks(count, step):
    return [pl.ds(i, step) for i in range(0, count, step)]


def at(index, count, step=32):
    return pl.ds(pl.multiple_of(index * count, step), count)


def prep_kernel(idx, w_ref, cot_ref, wo_ref, mine_ref, other_ref, sums_ref):
    k = idx[0]
    half = mine_ref.shape[1]
    for r in chunks(w_ref.shape[0], 32):
        wo_ref[r, :] = w_ref[r, :].astype(bf16)
    for r in chunks(cot_ref.shape[0], 32):
        v = cot_ref[r, :]
        sums_ref[r, :] = jnp.broadcast_to(jnp.sum(v, axis=1, keepdims=True), (32, 128))
        mine_ref[r, :] = cot_ref[r, at(k, half, 128)].astype(bf16)
        other_ref[r, :] = cot_ref[r, at(1 - k, half, 128)].astype(bf16)


def rest_kernel(last_ref, taps_ref, o_ref):
    for r in chunks(last_ref.shape[0], 32):
        o_ref[r, :D] = last_ref[r, :].astype(bf16)
        for j in range(KERNEL_TAPS):
            o_ref[r, D + j * INNER : D + (j + 1) * INNER] = taps_ref[j, r, :].astype(bf16)


def input_kernel(idx, tok_ref, gs_ref, hid_ref, hat_ref, slope_ref, scale_ref):
    for r in chunks(tok_ref.shape[0], 16):
        v = tok_ref[r, :]
        center = jnp.sum(v, axis=1, keepdims=True) * (1.0 / D)
        square = jnp.sum(v * v, axis=1, keepdims=True) * (1.0 / D)
        scale = lax.rsqrt(square - center * center + norm_eps)
        hat = (v - center) * scale
        hid, slope = gelu_pair(hat * gs_ref[0:1, :] + gs_ref[1:2, :])
        hid_ref[r, :] = hid.astype(bf16)
        hat_ref[r, :] = hat.astype(bf16)
        slope_ref[r, :] = slope.astype(bf16)
        scale_ref[r, :] = jnp.broadcast_to(scale, (16, 128))


def put_stats(ref, parts):
    for i, part in enumerate(parts):
        ref[i : i + 1, :] = part


def first_kernel(idx, own_ref, got_ref, hid_ref, cols_ref, w_ref, inner_ref, st_ref):
    k = idx[0]
    loc = own_ref.shape[0]
    w_ref[at(k, loc), :] = own_ref[...]
    w_ref[at(1 - k, loc), :] = got_ref[...]
    v = mul(w_ref[...], hid_ref[...], NT) + cols_ref[:, 0:1]
    inner_ref[...] = v
    put_stats(st_ref, (jnp.sum(v, axis=0, keepdims=True), jnp.sum(v * v, axis=0, keepdims=True)))


def center_scale(st_ref, got_ref):
    center = (st_ref[0:1, :] + got_ref[0:1, :]) * (1.0 / INNER)
    square = (st_ref[1:2, :] + got_ref[1:2, :]) * (1.0 / INNER)
    return center, lax.rsqrt(square - center * center + norm_eps)


def second_kernel(idx, inner_ref, st_ref, got_ref, cols_ref, valid_ref, hid_ref, hat_ref, slope_ref):
    center, scale = center_scale(st_ref, got_ref)
    valid = valid_ref[:, at(idx[0], hid_ref.shape[1], 128)].astype(f32)
    for r in chunks(inner_ref.shape[0], 32):
        hat = (inner_ref[r, :] - center) * scale
        hid, slope = gelu_pair(hat * cols_ref[r, 1:2] + cols_ref[r, 2:3])
        hid_ref[r, :] = (hid * valid).astype(bf16)
        hat_ref[r, :] = hat
        slope_ref[r, :] = slope * valid


def slabs_of(k, v_ref, row, in_ref, out_ref):
    half = v_ref.shape[1]
    rows = v_ref.shape[0]
    in_ref[row, :] = v_ref[:, at(1 - k, half - REACH, 128)]
    out_ref[row, :] = v_ref[:, at(k, half - REACH, 128)]


def slab_kernel(idx, own_ref, got_ref, in_ref, out_ref):
    k, y = idx[0], idx[1]
    wide = own_ref.shape[0]
    slabs_of(k, own_ref, at(y, wide), in_ref, out_ref)
    slabs_of(k, got_ref, at(1 - y, wide), in_ref, out_ref)


def fill_reach(k, ext_ref, in_ref, out_ref, half):
    @pl.when(k == 0)
    def _():
        ext_ref[:, :REACH] = out_ref[...]
        ext_ref[:, REACH + half :] = in_ref[...]

    @pl.when(k == 1)
    def _():
        ext_ref[:, :REACH] = in_ref[...]
        ext_ref[:, REACH + half :] = out_ref[...]


def conv_kernel(
    total, idx, lengths, own_ref, got_ref, in_ref, out_ref, wo_ref, wg_ref, cols_ref,
    ext_ref, inner_ref, st_ref, last_ref, taps_ref, mask_ref, stack,
):
    k, y = idx[0], idx[1]
    wide, half = own_ref.shape
    loc = wo_ref.shape[0]
    ext_ref[at(y, wide), REACH : REACH + half] = own_ref[...]
    ext_ref[at(1 - y, wide), REACH : REACH + half] = got_ref[...]
    fill_reach(k, ext_ref, in_ref, out_ref, half)
    last_ref[at(k, loc), :] = wo_ref[:, :D]
    last_ref[at(1 - k, loc), :] = wg_ref[:, :D]
    taps_ref[at(k, loc), :] = wo_ref[:, D:]
    taps_ref[at(1 - k, loc), :] = wg_ref[:, D:]
    positions = idx[5] - REACH + lax.broadcasted_iota(jnp.int32, (1, half + 2 * REACH), 1)
    segment = jnp.zeros_like(positions)
    bound = jnp.int32(0)
    for i in range(lengths.shape[0]):
        bound = bound + lengths[i]
        segment = segment + (positions >= bound).astype(jnp.int32)
    segment = jnp.where((positions >= 0) & (positions < total), segment, -1)
    centre = segment[:, REACH : REACH + half]
    for j in range(KERNEL_TAPS):
        lanes = slice(j * DILATION_SPAN, j * DILATION_SPAN + half)
        mask = (segment[:, lanes] == centre).astype(f32)
        mask_ref[j : j + 1, :] = mask
        low = mask.astype(bf16)
        for i in range(0, INNER, 160):
            stack[j * INNER + i : j * INNER + i + 160, :] = ext_ref[i : i + 160, lanes] * low
    v = mul(taps_ref[...], stack[...], NN) + cols_ref[:, 3:4]
    inner_ref[...] = v
    put_stats(st_ref, (jnp.sum(v, axis=0, keepdims=True), jnp.sum(v * v, axis=0, keepdims=True)))


def cotangent_kernel(idx, last_ref, mine_ref, sib_ref, opp_ref, diag_ref, gw_ref, g_ref):
    k, y = idx[0], idx[1]
    col = mine_ref.shape[0]
    gw_ref[at(2 * y + k, col), :] = mine_ref[...]
    gw_ref[at(2 * y + 1 - k, col), :] = sib_ref[...]
    gw_ref[at(2 * (1 - y) + k, col), :] = opp_ref[...]
    gw_ref[at(2 * (1 - y) + 1 - k, col), :] = diag_ref[...]
    g_ref[...] = mul(last_ref[...], gw_ref[...], NN)


def third_kernel(inner_ref, st_ref, got_ref, cols_ref, g_ref, hid_ref, e_ref, hat_ref, part_ref):
    center, scale = center_scale(st_ref, got_ref)
    plain = jnp.zeros_like(center)
    cross = jnp.zeros_like(center)
    for r in chunks(inner_ref.shape[0], 32):
        hat = (inner_ref[r, :] - center) * scale
        gain = cols_ref[r, 4:5]
        hid, slope = gelu_pair(hat * gain + cols_ref[r, 5:6])
        hid_ref[r, :] = hid.astype(bf16)
        hat_ref[r, :] = hat
        e = slope * g_ref[r, :]
        e_ref[r, :] = e
        eg = e * gain
        plain = plain + jnp.sum(eg, axis=0, keepdims=True)
        cross = cross + jnp.sum(eg * hat, axis=0, keepdims=True)
    put_stats(part_ref, (plain, cross, scale))


def norm_back(r, e_ref, hat_ref, part_ref, got_ref, scale, gain, sums_ref):
    plain = (part_ref[0:1, :] + got_ref[0:1, :]) * (1.0 / INNER)
    cross = (part_ref[1:2, :] + got_ref[1:2, :]) * (1.0 / INNER)
    e, hat = e_ref[r, :], hat_ref[r, :]
    grad = scale * (e * gain - plain - hat * cross)
    sums_ref[r, 0:1] = jnp.sum(e * hat, axis=1, keepdims=True)
    sums_ref[r, 1:2] = jnp.sum(e, axis=1, keepdims=True)
    sums_ref[r, 2:3] = jnp.sum(grad, axis=1, keepdims=True)
    return grad


def third_back_kernel(idx, e_ref, hat_ref, part_ref, got_ref, cols_ref, dz_ref, in_ref, out_ref, sums_ref):
    for r in chunks(e_ref.shape[0], 32):
        grad = norm_back(r, e_ref, hat_ref, part_ref, got_ref, part_ref[2:3, :], cols_ref[r, 4:5], sums_ref)
        dz_ref[r, :] = grad.astype(bf16)
    slabs_of(idx[0], dz_ref, slice(None), in_ref, out_ref)


def split_rows(k, full, own_ref, send_ref, lanes):
    loc = own_ref.shape[0]
    own_ref[:, lanes] = full[at(k, loc), lanes]
    send_ref[:, lanes] = full[at(1 - k, loc), lanes].astype(bf16)


def grads_kernel(idx, dz_ref, ext_ref, mask_ref, hid_ref, gw_ref, own_ref, send_ref, full):
    k = idx[0]
    half = dz_ref.shape[1]
    full[:, :D] = mul(hid_ref[...], gw_ref[...], NT)
    split_rows(k, full, own_ref, send_ref, slice(0, D))
    for j in range(KERNEL_TAPS):
        masked = dz_ref[...] * mask_ref[j : j + 1, :].astype(bf16)
        moved = ext_ref[:, j * DILATION_SPAN : j * DILATION_SPAN + half]
        lanes = slice(D + j * INNER, D + (j + 1) * INNER)
        full[:, lanes] = mul(masked, moved, NT)
        split_rows(k, full, own_ref, send_ref, lanes)


def conv_back_kernel(idx, dz_ref, in_ref, out_ref, mask_ref, taps_ref, own_ref, send_ref, ext, full):
    k, y = idx[0], idx[1]
    wide, half = dz_ref.shape
    ext[:, REACH : REACH + half] = dz_ref[...]
    fill_reach(k, ext, in_ref, out_ref, half)
    total = None
    for j in range(KERNEL_TAPS):
        begin = REACH - (j - KERNEL_TAPS // 2) * DILATION_SPAN
        mask = mask_ref[KERNEL_TAPS - 1 - j : KERNEL_TAPS - j, :].astype(bf16)
        part = mul(taps_ref[:, j * INNER : (j + 1) * INNER], ext[:, begin : begin + half] * mask, TN)
        total = part if total is None else total + part
    full[...] = total
    own_ref[...] = full[at(y, wide), :]
    send_ref[...] = full[at(1 - y, wide), :].astype(bf16)


def second_back_kernel(own_ref, got_ref, slope_ref, hat_ref, cols_ref, e_ref, part_ref):
    plain = jnp.zeros((1, own_ref.shape[1]), f32)
    cross = jnp.zeros_like(plain)
    for r in chunks(own_ref.shape[0], 32):
        e = slope_ref[r, :] * (own_ref[r, :] + got_ref[r, :].astype(f32))
        e_ref[r, :] = e
        eg = e * cols_ref[r, 1:2]
        plain = plain + jnp.sum(eg, axis=0, keepdims=True)
        cross = cross + jnp.sum(eg * hat_ref[r, :], axis=0, keepdims=True)
    put_stats(part_ref, (plain, cross))


def first_back_kernel(
    idx, e_ref, hat_ref, part_ref, got_ref, st_ref, stg_ref, cols_ref, hid_ref,
    dz_ref, own_ref, send_ref, sums_ref, full,
):
    _, scale = center_scale(st_ref, stg_ref)
    for r in chunks(e_ref.shape[0], 32):
        grad = norm_back(r, e_ref, hat_ref, part_ref, got_ref, scale, cols_ref[r, 1:2], sums_ref)
        dz_ref[r, :] = grad.astype(bf16)
    full[...] = mul(dz_ref[...], hid_ref[...], NN)
    split_rows(idx[0], full, own_ref, send_ref, slice(0, D))


def halves_kernel(idx, z_ref, w_ref, own_ref, send_ref, full):
    y = idx[1]
    full[...] = mul(z_ref[...], w_ref[...], TN)
    for r in chunks(full.shape[0], 64):
        own_ref[r, :] = full[r, at(y, HALF_D, 128)]
        send_ref[r, :] = full[r, at(1 - y, HALF_D, 128)].astype(bf16)


def column_halves(k, flipped, mine_ref, send_ref, full):
    col = mine_ref.shape[0]
    full[...] = flipped
    mine_ref[...] = full[at(k, col), :]
    send_ref[...] = full[at(1 - k, col), :]


def output_kernel(idx, own_ref, got_ref, tok_ref, bias_ref, valid_ref, mine_ref, send_ref, sq_ref, full):
    k, y = idx[0], idx[1]
    half = own_ref.shape[0]
    bias = bias_ref[:, at(y, HALF_D, 128)]
    branch = own_ref[...] + got_ref[...].astype(f32) + bias
    out = tok_ref[...] + branch
    valid = valid_ref[:, at(k, half, 128)].astype(f32)
    sq_ref[0:1, :] = jnp.sum(valid * mul_rows(out), axis=1, keepdims=True) * jnp.ones((1, 128), f32)
    sq_ref[1:2, :] = jnp.sum(valid * mul_rows(branch), axis=1, keepdims=True) * jnp.ones((1, 128), f32)
    sq_ref[2:3, :] = jnp.sum(valid, axis=1, keepdims=True) * jnp.full((1, 128), 0.5, f32)
    sq_ref[3:8, :] = jnp.zeros((5, 128), f32)
    column_halves(k, out.T, mine_ref, send_ref, full)


def mul_rows(v):
    rows = jnp.sum(v * v, axis=1, keepdims=True)
    return jnp.broadcast_to(rows, (v.shape[0], 128)).T[0:1, :]


def token_kernel(idx, own_ref, got_ref, slope_ref, hat_ref, gs_ref, e_ref, part_ref, sums_ref):
    y = idx[1]
    cols = at(y, HALF_D, 128)
    gain = gs_ref[0:1, cols]
    sum_cross = jnp.zeros((1, HALF_D), f32)
    sum_plain = jnp.zeros((1, HALF_D), f32)
    for r in chunks(own_ref.shape[0], 32):
        e = slope_ref[r, cols].astype(f32) * (own_ref[r, :] + got_ref[r, :].astype(f32))
        hat = hat_ref[r, cols].astype(f32)
        eg = e * gain
        e_ref[r, :] = eg
        part_ref[r, 0:1] = jnp.sum(eg, axis=1, keepdims=True)
        part_ref[r, 1:2] = jnp.sum(eg * hat, axis=1, keepdims=True)
        sum_cross = sum_cross + jnp.sum(e * hat, axis=0, keepdims=True)
        sum_plain = sum_plain + jnp.sum(e, axis=0, keepdims=True)
    put_stats(sums_ref, (sum_cross, sum_plain))


def flip_kernel(part_ref, o_ref):
    o_ref[...] = part_ref[...].T[0:8, :]


def token_back_kernel(idx, e_ref, hat_ref, scale_ref, part_ref, got_ref, mine_ref, send_ref, rows, full):
    cols = at(idx[1], HALF_D, 128)
    means = ((part_ref[...] + got_ref[...]) * (1.0 / D)).T
    for r in range(0, e_ref.shape[0], 64):
        s = slice(r, r + 64)
        hat = hat_ref[s, cols].astype(f32)
        rows[s, :] = scale_ref[s, 0:1] * (e_ref[s, :] - means[s, 0:1] - hat * means[s, 1:2])
    column_halves(idx[0], rows[...].T, mine_ref, send_ref, full)


def place_kernel(idx, mine_ref, got_ref, o_ref):
    half = mine_ref.shape[1]
    o_ref[:, at(idx[0], half, 128)] = mine_ref[...]
    o_ref[:, at(1 - idx[0], half, 128)] = got_ref[...]


def place_add_kernel(idx, mine_ref, got_ref, base_ref, o_ref):
    half = mine_ref.shape[1]
    mine, other = at(idx[0], half, 128), at(1 - idx[0], half, 128)
    o_ref[:, mine] = base_ref[:, mine] + mine_ref[...]
    o_ref[:, other] = base_ref[:, other] + got_ref[...]


TAIL = INNER // 2


def early_columns(b):
    taps = D
    return (
        (taps + b * INNER, INNER),
        (b * INNER, INNER),
        (taps + (2 + b) * INNER, INNER),
        (taps + 4 * INNER + b * TAIL, TAIL),
    )


def pair_kernel(idx, own_ref, got_ref, keep_ref, send_ref):
    for b in range(2):

        @pl.when(idx[2] == b)
        def _():
            to = 0
            for (mine, count), (other, _n) in zip(early_columns(b), early_columns(1 - b)):
                for r in chunks(own_ref.shape[0], 32):
                    keep_ref[r, to : to + count] = own_ref[r, mine : mine + count] + got_ref[
                        r, mine : mine + count
                    ].astype(f32)
                    send_ref[r, to : to + count] = (
                        own_ref[r, other : other + count] + got_ref[r, other : other + count].astype(f32)
                    ).astype(bf16)
                to += count


def across_x_kernel(idx, keep_ref, got_ref, sum_ref, send_ref):
    for r in chunks(keep_ref.shape[0], 32):
        sum_ref[r, :] = keep_ref[r, :] + got_ref[r, :].astype(f32)

    @pl.when(idx[3] % 2 == 0)
    def _():
        send_ref[:, : INNER + TAIL] = sum_ref[:, 2 * INNER :].astype(bf16)
        send_ref[:, INNER + TAIL :] = jnp.zeros_like(send_ref[:, INNER + TAIL :])

    @pl.when(idx[3] % 2 == 1)
    def _():
        send_ref[...] = sum_ref[:, : 2 * INNER].astype(bf16)


def along_z_kernel(idx, sum_ref, got_ref, keep_ref, send_ref):
    h = idx[3]

    @pl.when(h % 2 == 0)
    def _():
        for q in range(2):

            @pl.when(h // 2 % 2 == q)
            def _():
                mine = slice(q * INNER, (q + 1) * INNER)
                other = slice((1 - q) * INNER, (2 - q) * INNER)
                keep_ref[:, :INNER] = sum_ref[:, mine] + got_ref[:, mine].astype(f32)
                send_ref[:, :INNER] = (sum_ref[:, other] + got_ref[:, other].astype(f32)).astype(bf16)

        keep_ref[:, INNER:] = jnp.zeros_like(keep_ref[:, INNER:])
        send_ref[:, INNER:] = jnp.zeros_like(send_ref[:, INNER:])

    @pl.when(h % 2 == 1)
    def _():
        v = sum_ref[:, 2 * INNER :] + got_ref[:, : INNER + TAIL].astype(f32)
        keep_ref[...] = v
        send_ref[...] = v.astype(bf16)


def own_kernel(idx, first_ref, taps_ref, last_ref, unit_ref):
    h, b = idx[3], idx[2]
    unit_ref[:, INNER:] = jnp.zeros_like(unit_ref[:, INNER:])
    for i in range(2):

        @pl.when((h == 0) & (b == i))
        def _():
            unit_ref[:, :INNER] = taps_ref[i]

        @pl.when((h == 1) & (b == i))
        def _():
            unit_ref[:, :INNER] = first_ref[:, i * INNER : (i + 1) * INNER]

        @pl.when((h == 2) & (b == i))
        def _():
            unit_ref[:, :INNER] = last_ref[:, i * INNER : (i + 1) * INNER]

        @pl.when((h == 3) & (b == i))
        def _():
            unit_ref[:, :INNER] = taps_ref[2 + i]
            unit_ref[:, INNER:] = taps_ref[4, :, i * TAIL : (i + 1) * TAIL]

    @pl.when(h > 3)
    def _():
        unit_ref[...] = jnp.zeros_like(unit_ref)


def finish_kernel(idx, keep_ref, got_ref, head_ref, head_got_ref, old_ref, sum_ref, new_ref, cross_ref):
    h = idx[3]

    @pl.when(h == 1)
    def _():
        v = head_ref[...] + head_got_ref[...].astype(f32)
        sum_ref[:, :INNER] = v.astype(bf16)
        sum_ref[:, INNER:] = jnp.zeros_like(sum_ref[:, INNER:])
        new_ref[:, :INNER] = (muon_keep * old_ref[:, :INNER] + v).astype(bf16)
        new_ref[:, INNER:] = jnp.zeros_like(new_ref[:, INNER:])

    @pl.when(h != 1)
    def _():
        v = keep_ref[...] + got_ref[...].astype(f32)
        sum_ref[...] = v.astype(bf16)
        new_ref[...] = (muon_keep * old_ref[...] + v).astype(bf16)

    @pl.when(h == 3)
    def _():
        cross_ref[:, :TAIL] = new_ref[:, INNER:]
        cross_ref[:, TAIL:] = new_ref[:, INNER:]

    @pl.when(h != 3)
    def _():
        cross_ref[...] = new_ref[:, :INNER]


def block_kernel(idx, new_ref, got_ref, o_ref):
    h, b = idx[3], idx[2]
    long = (h == 1) | (h == 2)
    for i in range(2):

        @pl.when(long & (b == i))
        def _():
            o_ref[:, i * INNER : (i + 1) * INNER] = new_ref[:, :INNER]
            o_ref[:, (1 - i) * INNER : (2 - i) * INNER] = got_ref[...]

        @pl.when(jnp.logical_not(long) & (b == i))
        def _():
            o_ref[:, :INNER] = new_ref[:, :INNER]
            o_ref[:, INNER + i * TAIL : INNER + (i + 1) * TAIL] = new_ref[:, INNER:]
            o_ref[:, INNER + (1 - i) * TAIL : INNER + (2 - i) * TAIL] = got_ref[:, :TAIL]


def ortho_kernel(
    coarse, fine, idx, own_ref, sib_ref, opp_ref, diag_ref, mine_ref, theirs_ref,
    X, Xh, Xl, A, Ah, Al, Ph,
):
    R, C = X.shape
    k, y, h = idx[0], idx[1], idx[3]
    loc = own_ref.shape[0]
    MT = R // 2
    long = (h == 1) | (h == 2)
    fifth = (h == 3) & (k == 1)
    for place, ref in (
        (2 * y + k, own_ref),
        (2 * y + 1 - k, sib_ref),
        (2 * (1 - y) + k, opp_ref),
        (2 * (1 - y) + 1 - k, diag_ref),
    ):

        @pl.when(long)
        def _():
            X[at(place, loc), :] = ref[...].astype(f32)

        @pl.when(jnp.logical_not(long))
        def _():
            X[at(place, loc), INNER:] = jnp.zeros((loc, C - INNER), f32)

        @pl.when(jnp.logical_not(long) & jnp.logical_not(fifth))
        def _():
            X[at(place, loc), :INNER] = ref[:, :INNER].astype(f32)

        @pl.when(fifth)
        def _():
            X[at(place, loc), :INNER] = ref[:, INNER:].astype(f32)

    def square(i, acc):
        v = X[pl.ds(i * 16, 16), :]
        v = v * v
        return acc + v[:8] + v[8:]

    total = jnp.sum(lax.fori_loop(0, R // 16, square, jnp.zeros((8, C), f32)))
    inverse = 1.0 / (jnp.sqrt(total) + 1e-07)

    def scaled(i, _):
        r = pl.ds(i * 64, 64)
        X[r, :] = X[r, :] * inverse
        return 0

    lax.fori_loop(0, R // 64, scaled, 0)

    def split(low):
        def step(i, _):
            r = pl.ds(i * 32, 32)
            v = X[r, :]
            Xh[r, :] = v.astype(bf16)
            if low:
                Xl[r, :] = (v - Xh[r, :].astype(f32)).astype(bf16)
            return 0

        lax.fori_loop(0, R // 32, step, 0)

    def sweep_coarse(_, __):
        split(False)

        def gram(i, _):
            r = pl.ds(i * MT, MT)
            a = mul(Xh[r, :], Xh[...], NT)
            A[r, :] = a
            Ah[r, :] = a.astype(bf16)
            return 0

        lax.fori_loop(0, R // MT, gram, 0)

        def poly(i, _):
            r = pl.ds(i * MT, MT)
            Ph[r, :] = (coef_second * A[r, :] + coef_third * mul(Ah[r, :], Ah[...], NN)).astype(bf16)
            return 0

        lax.fori_loop(0, R // MT, poly, 0)

        def update(i, _):
            r = pl.ds(i * MT, MT)
            X[r, :] = coef_first * X[r, :] + mul(Ph[r, :], Xh[...], NN)
            return 0

        lax.fori_loop(0, R // MT, update, 0)
        return 0

    def sweep_fine(_, __):
        split(True)

        def gram(i, _):
            r = pl.ds(i * MT, MT)
            a = mul(Xh[r, :], Xh[...], NT) + (mul(Xh[r, :], Xl[...], NT) + mul(Xl[r, :], Xh[...], NT))
            A[r, :] = a
            Ah[r, :] = a.astype(bf16)
            Al[r, :] = (a - Ah[r, :].astype(f32)).astype(bf16)
            return 0

        lax.fori_loop(0, R // MT, gram, 0)

        def poly(i, _):
            r = pl.ds(i * MT, MT)
            p = coef_second * A[r, :] + coef_third * (
                mul(Ah[r, :], Ah[...], NN) + (mul(Ah[r, :], Al[...], NN) + mul(Al[r, :], Ah[...], NN))
            )
            Ph[r, :] = p.astype(bf16)
            A[r, :] = p - Ph[r, :].astype(f32)
            return 0

        lax.fori_loop(0, R // MT, poly, 0)

        def update(i, _):
            r = pl.ds(i * MT, MT)
            low = A[r, :].astype(bf16)
            X[r, :] = (
                coef_first * X[r, :]
                + mul(Ph[r, :], Xh[...], NN)
                + (mul(Ph[r, :], Xl[...], NN) + mul(low, Xh[...], NN))
            )
            return 0

        lax.fori_loop(0, R // MT, update, 0)
        return 0

    lax.fori_loop(0, coarse, sweep_coarse, 0)
    lax.fori_loop(0, fine, sweep_fine, 0)
    mine_ref[...] = X[at(2 * y + k, loc), :].astype(bf16)
    theirs_ref[...] = X[at(2 * y + 1 - k, loc), :INNER].astype(bf16)


def step_kernel(idx, mine_ref, got_ref, o_ref):
    h, b, k = idx[3], idx[2], idx[0]

    @pl.when((h == 0) | ((h == 3) & (k == 0)))
    def _():
        o_ref[:, :INNER] = mine_ref[:, :INNER]

    @pl.when((h == 3) & (k == 1))
    def _():
        o_ref[:, :INNER] = got_ref[...]

    for i in range(2):

        @pl.when(((h == 1) | (h == 2)) & (b == i))
        def _():
            o_ref[:, :INNER] = mine_ref[:, i * INNER : (i + 1) * INNER]

        @pl.when((h == 3) & (k == 0) & (b == i))
        def _():
            o_ref[:, INNER:] = got_ref[:, i * TAIL : (i + 1) * TAIL]

        @pl.when((h == 3) & (k == 1) & (b == i))
        def _():
            o_ref[:, INNER:] = mine_ref[:, i * TAIL : (i + 1) * TAIL]

    @pl.when(h != 3)
    def _():
        o_ref[:, INNER:] = jnp.zeros_like(o_ref[:, INNER:])

    @pl.when(h > 3)
    def _():
        o_ref[:, :INNER] = jnp.zeros_like(o_ref[:, :INNER])


def join_kernel(idx, own_ref, got_ref, o_ref):
    h = idx[3]
    for q in range(2):

        @pl.when(h // 2 % 2 == q)
        def _():
            o_ref[:, q * INNER : (q + 1) * INNER] = own_ref[:, :INNER]
            o_ref[:, (1 - q) * INNER : (2 - q) * INNER] = got_ref[:, :INNER]
            o_ref[:, 2 * INNER :] = (own_ref if q else got_ref)[:, INNER:]


def apply_kernel(
    keep, rate_long, rate_tap, idx, own_ref, x_ref, z_ref, zx_ref, first_ref, taps_ref, last_ref,
    of_ref, ot_ref, ol_ref,
):
    h, b = idx[3], idx[2]
    for odd in range(2):
        for i in range(2):

            @pl.when((h % 2 == odd) & (b == i))
            def _():
                even = (own_ref, x_ref) if odd == 0 else (z_ref, zx_ref)
                odds = (z_ref, zx_ref) if odd == 0 else (own_ref, x_ref)
                for r in chunks(first_ref.shape[0], 32):
                    for q in range(2):
                        e = even[q ^ i]
                        o = odds[q ^ i]
                        lanes = slice(q * INNER, (q + 1) * INNER)
                        tail = slice(q * TAIL, (q + 1) * TAIL)
                        of_ref[r, lanes] = keep * first_ref[r, lanes] + rate_long * o[r, :INNER].astype(f32)
                        ol_ref[r, lanes] = keep * last_ref[r, lanes] + rate_long * e[r, INNER : 2 * INNER].astype(f32)
                        ot_ref[q, r, :] = keep * taps_ref[q, r, :] + rate_tap * e[r, :INNER].astype(f32)
                        ot_ref[2 + q, r, :] = keep * taps_ref[2 + q, r, :] + rate_tap * o[
                            r, INNER : 2 * INNER
                        ].astype(f32)
                        ot_ref[4, r, tail] = keep * taps_ref[4, r, tail] + rate_tap * o[r, 2 * INNER :].astype(f32)


def body(
    tokens,
    cotangent,
    lengths,
    valid_mask,
    weight_first,
    weight_dilated,
    weight_last,
    momentum_first,
    momentum_dilated,
    momentum_last,
    vector_params,
    vector_moment,
    vector_square,
):
    C = lax.axis_size("ch")
    S = lax.axis_size("seq")
    c = lax.axis_index("ch")
    s = lax.axis_index("seq")
    k = c % 2
    y = c // 2
    T = tokens.shape[0]
    half = T // 2
    loc = weight_first.shape[1]
    wide = 2 * loc
    col = D // C
    H = S // 2
    b = s % 2
    h = s // 2
    idx = jnp.stack([k, y, b, h, s, s * T + k * half]).astype(jnp.int32)

    sib = [(i, i ^ 1) for i in range(C)]
    opp = [(i, i ^ 2) for i in range(C)]
    diag = [(i, i ^ 3) for i in range(C)]
    xsw = [(i, i ^ 1) for i in range(S)]

    def swap_core(v):
        return lax.ppermute(v, "ch", sib)

    def swap_y(v):
        return lax.ppermute(v, "ch", opp)

    def swap_x(v):
        return lax.ppermute(v, "seq", xsw)

    def along_h(v, pairs):
        return lax.ppermute(v, "seq", [(2 * i + q, 2 * j + q) for i, j in pairs for q in range(2)])

    outer_pairs = []
    for i in range(S):
        for j in range(C):
            if j % 2 == 0 and i >= 1:
                outer_pairs.append((i * C + j, (i - 1) * C + (j ^ 1)))
            if j % 2 == 1 and i + 1 < S:
                outer_pairs.append((i * C + j, (i + 1) * C + (j ^ 1)))

    def swap_outer(v):
        return lax.ppermute(v, ("seq", "ch"), outer_pairs)

    w_first, w_taps, w_last = weight_first.T, jnp.swapaxes(weight_dilated, 1, 2), weight_last
    m_first, m_taps, m_last = momentum_first.T, jnp.swapaxes(momentum_dilated, 1, 2), momentum_last
    cot = cotangent.T
    valid = valid_mask.reshape(1, T)
    gain_shift = vector_params[: 2 * D].reshape(2, D)
    inner_rows = vector_params[2 * D : 2 * D + 6 * INNER].reshape(6, INNER)
    cols = lax.dynamic_slice_in_dim(inner_rows, y * wide, wide, 1).T
    bias_three = vector_params[2 * D + 6 * INNER :].reshape(1, D)

    low_first, cot_mine, cot_other, cot_sums = call(
        prep_kernel,
        [((loc, D), bf16), ((col, half), bf16), ((col, half), bf16), ((col, 128), f32)],
        [idx],
        [w_first, cot],
    )
    got_first = swap_core(low_first)
    cot_opp = swap_y(cot_mine)
    cot_sib = swap_core(cot_other)
    cot_diag = lax.ppermute(cot_other, "ch", diag)

    rows = 128
    steps = half // rows
    hid_one, hat_one, slope_one, scale_one = pl.pallas_call(
        input_kernel,
        out_shape=[
            jax.ShapeDtypeStruct((half, D), bf16),
            jax.ShapeDtypeStruct((half, D), bf16),
            jax.ShapeDtypeStruct((half, D), bf16),
            jax.ShapeDtypeStruct((half, 128), f32),
        ],
        grid_spec=pltpu.PrefetchScalarGridSpec(
            num_scalar_prefetch=1,
            grid=(steps,),
            in_specs=[
                pl.BlockSpec((rows, D), lambda i, idx: (idx[0] * steps + i, 0)),
                pl.BlockSpec((2, D), lambda i, idx: (0, 0)),
            ],
            out_specs=[
                pl.BlockSpec((rows, D), lambda i, idx: (i, 0)),
                pl.BlockSpec((rows, D), lambda i, idx: (i, 0)),
                pl.BlockSpec((rows, D), lambda i, idx: (i, 0)),
                pl.BlockSpec((rows, 128), lambda i, idx: (i, 0)),
            ],
        ),
        compiler_params=pltpu.CompilerParams(vmem_limit_bytes=24 * MIB),
        cost_estimate=pl.CostEstimate(flops=5 * 10**9, bytes_accessed=8 * 10**6, transcendentals=10**6),
    )(idx, tokens, gain_shift)

    (low_rest,) = call(rest_kernel, [((loc, D + KERNEL_TAPS * INNER), bf16)], [], [w_last, w_taps])
    got_rest = swap_core(low_rest)

    full_first, inner_one, st_two = call(
        first_kernel,
        [((wide, D), bf16), ((wide, half), f32), ((8, half), f32)],
        [idx],
        [low_first, got_first, hid_one, cols],
    )
    st_two_got = swap_y(st_two)
    hid_two, hat_two, slope_two = call(
        second_kernel,
        [((wide, half), bf16), ((wide, half), f32), ((wide, half), f32)],
        [idx],
        [inner_one, st_two, st_two_got, cols, valid],
    )
    hid_two_got = swap_y(hid_two)
    slab_in, slab_out = call(
        slab_kernel, [((INNER, REACH), bf16)] * 2, [idx], [hid_two, hid_two_got]
    )
    got_in, got_out = swap_core(slab_in), swap_outer(slab_out)
    ext, inner_two, st_three, full_last, full_taps, masks = call(
        functools.partial(conv_kernel, S * T),
        [
            ((INNER, half + 2 * REACH), bf16),
            ((wide, half), f32),
            ((8, half), f32),
            ((wide, D), bf16),
            ((wide, KERNEL_TAPS * INNER), bf16),
            ((8, half), f32),
        ],
        [idx, lengths],
        [hid_two, hid_two_got, got_in, got_out, low_rest, got_rest, cols],
        scratch=[((KERNEL_TAPS * INNER, half), bf16)],
        flops=10**9,
    )
    st_three_got = swap_y(st_three)
    gw, g_three = call(
        cotangent_kernel,
        [((D, half), bf16), ((wide, half), f32)],
        [idx],
        [full_last, cot_mine, cot_sib, cot_opp, cot_diag],
        flops=4 * 10**8,
    )
    hid_three, e_three, hat_three, part_three = call(
        third_kernel,
        [((wide, half), bf16), ((wide, half), f32), ((wide, half), f32), ((8, half), f32)],
        [],
        [inner_two, st_three, st_three_got, cols, g_three],
    )
    part_three_got = swap_y(part_three)
    dz_two, slab_in, slab_out, sums_three = call(
        third_back_kernel,
        [((wide, half), bf16), ((wide, REACH), bf16), ((wide, REACH), bf16), ((wide, 8), f32)],
        [idx],
        [e_three, hat_three, part_three, part_three_got, cols],
    )
    got_in, got_out = swap_core(slab_in), swap_outer(slab_out)
    early_size = D + KERNEL_TAPS * INNER
    early_own, early_send = call(
        grads_kernel,
        [((loc, early_size), f32), ((loc, early_size), bf16)],
        [idx],
        [dz_two, ext, masks, hid_three, gw],
        scratch=[((wide, early_size), f32)],
        flops=16 * 10**8,
        limit=32,
    )
    early_got = swap_core(early_send)
    back_own, back_send = call(
        conv_back_kernel,
        [((wide, half), f32), ((wide, half), bf16)],
        [idx],
        [dz_two, got_in, got_out, masks, full_taps],
        scratch=[((wide, half + 2 * REACH), bf16), ((INNER, half), f32)],
        flops=10**9,
    )
    back_got = swap_y(back_send)
    early = 3 * INNER + TAIL
    keep, send = call(
        pair_kernel, [((loc, early), f32), ((loc, early), bf16)], [idx], [early_own, early_got]
    )
    x_got = swap_x(send)
    e_two, part_two = call(
        second_back_kernel,
        [((wide, half), f32), ((8, half), f32)],
        [],
        [back_own, back_got, slope_two, hat_two, cols],
    )
    part_two_got = swap_y(part_two)
    dz_one, first_own, first_send, sums_two = call(
        first_back_kernel,
        [((wide, half), bf16), ((loc, D), f32), ((loc, D), bf16), ((wide, 8), f32)],
        [idx],
        [e_two, hat_two, part_two, part_two_got, st_two, st_two_got, cols, hid_one],
        scratch=[((wide, D), f32)],
        flops=4 * 10**8,
    )
    first_got = swap_core(first_send)

    first_pair = first_own + first_got.astype(f32)
    head = lax.dynamic_slice_in_dim(first_pair, b * INNER, INNER, 1)
    head_send = lax.dynamic_slice_in_dim(first_pair, (1 - b) * INNER, INNER, 1).astype(bf16)
    head = head + swap_x(head_send).astype(f32)

    early_sum, send = call(
        across_x_kernel, [((loc, early), f32), ((loc, 2 * INNER), bf16)], [idx], [keep, x_got]
    )
    span = H
    while span > 4:
        span //= 2
        fold = [(i + span, i) for i in range(span)]
        early_sum = early_sum + along_h(early_sum.astype(bf16), fold).astype(f32)
        head = head + along_h(head.astype(bf16), fold).astype(f32)
        even = jnp.concatenate([early_sum[:, 2 * INNER :], jnp.zeros((loc, TAIL), f32)], axis=1)
        send = jnp.where(h % 2 == 0, even, early_sum[:, : 2 * INNER]).astype(bf16)
    z_got = along_h(send, [(i, i ^ 1) for i in range(4)])
    head = head + along_h(head.astype(bf16), [(0, 1), (2, 3)]).astype(f32)
    keep, send = call(
        along_z_kernel,
        [((loc, INNER + TAIL), f32), ((loc, INNER + TAIL), bf16)],
        [idx],
        [early_sum, z_got],
    )
    z_got = along_h(send, [(i, i ^ 2) for i in range(4)])
    head_got = along_h(head.astype(bf16), [(3, 1)])
    (old_unit,) = call(own_kernel, [((loc, INNER + TAIL), f32)], [idx], [m_first, m_taps, m_last])
    sum_unit, new_unit, cross = call(
        finish_kernel,
        [((loc, INNER + TAIL), bf16), ((loc, INNER + TAIL), bf16), ((loc, INNER), bf16)],
        [idx],
        [keep, z_got, head, head_got, old_unit],
    )
    cross_got = swap_x(cross)
    (block,) = call(block_kernel, [((loc, D), bf16)], [idx], [new_unit, cross_got])
    block_sib, block_opp = swap_core(block), swap_y(block)
    block_diag = swap_core(block_opp)

    def gather(unit):
        got = along_h(unit, [(i, i ^ 2) for i in range(4)])
        (joined,) = call(join_kernel, [((loc, 2 * INNER + TAIL), bf16)], [idx], [unit, got])
        joined_x = swap_x(joined)
        other = along_h(joined, [(i, i ^ 1) for i in range(4)])
        other_x = swap_x(other)
        result = [joined, joined_x, other, other_x]
        span = 4
        while span < H:
            spread = [(i, i + span) for i in range(span)]
            result = [jnp.where((h >= span) & (h < 2 * span), along_h(v, spread), v) for v in result]
            span *= 2
        return result

    def apply(keep, rate_long, rate_tap, parts, first, taps, last):
        return call(
            functools.partial(apply_kernel, keep, rate_long, rate_tap),
            [((loc, D), f32), ((KERNEL_TAPS, loc, INNER), f32), ((loc, D), f32)],
            [idx],
            [*parts, first, taps, last],
            limit=32,
        )

    new_first, new_taps, new_last = apply(muon_keep, 1.0, 1.0, gather(sum_unit), m_first, m_taps, m_last)

    mine, theirs = call(
        functools.partial(ortho_kernel, 3, 2),
        [((loc, D), bf16), ((loc, INNER), bf16)],
        [idx],
        [block, block_sib, block_opp, block_diag],
        scratch=[
            ((INNER, D), f32),
            ((INNER, D), bf16),
            ((INNER, D), bf16),
            ((INNER, INNER), f32),
            ((INNER, INNER), bf16),
            ((INNER, INNER), bf16),
            ((INNER, INNER), bf16),
        ],
        limit=32,
        flops=30 * 10**9,
    )
    theirs_got = swap_core(theirs)
    (step_unit,) = call(step_kernel, [((loc, INNER + TAIL), bf16)], [idx], [mine, theirs_got])
    keep_weight = 1.0 - muon_rate * decay_rate
    rate = muon_rate * muon_scale
    out_first, out_taps, out_last = apply(
        keep_weight,
        -rate * math.sqrt(D),
        -rate * math.sqrt(INNER),
        gather(step_unit),
        w_first,
        w_taps,
        w_last,
    )

    half_out = [((half, HALF_D), f32), ((half, HALF_D), bf16)]
    branch_own, branch_send = call(
        halves_kernel, half_out, [idx], [hid_three, full_last], scratch=[((half, D), f32)], flops=4 * 10**8
    )
    branch_got = swap_y(branch_send)
    own_tokens = lax.dynamic_slice(tokens, (k * half, y * HALF_D), (half, HALF_D))
    out_mine, out_send, squares = call(
        output_kernel,
        [((col, half), f32), ((col, half), f32), ((8, 128), f32)],
        [idx],
        [branch_own, branch_got, own_tokens, bias_three, valid],
        scratch=[((HALF_D, half), f32)],
    )
    (block_output,) = call(place_kernel, [((col, T), f32)], [idx], [out_mine, swap_core(out_send)])

    back_own, back_send = call(
        halves_kernel, half_out, [idx], [dz_one, full_first], scratch=[((half, D), f32)], flops=4 * 10**8
    )
    back_got = swap_y(back_send)
    e_one, part_one, sums_one = call(
        token_kernel,
        [((half, HALF_D), f32), ((half, 128), f32), ((8, HALF_D), f32)],
        [idx],
        [back_own, back_got, slope_one, hat_one, gain_shift],
    )
    (part_one,) = call(flip_kernel, [((8, half), f32)], [], [part_one])
    grad_mine, grad_send = call(
        token_back_kernel,
        [((col, half), f32), ((col, half), f32)],
        [idx],
        [e_one, hat_one, scale_one, part_one, swap_y(part_one)],
        scratch=[((half, HALF_D), f32), ((HALF_D, half), f32)],
    )
    (tokens_grad,) = call(
        place_add_kernel, [((col, T), f32)], [idx], [grad_mine, swap_core(grad_send), cot]
    )

    grid = jnp.zeros((6, INNER), f32)
    inner = jnp.concatenate([sums_two[:, 2:3], sums_two[:, 0:2], sums_three[:, 2:3], sums_three[:, 0:2]], axis=1)
    grid = lax.dynamic_update_slice(grid, inner.T, (0, y * wide))
    ones = jnp.zeros((2, D), f32)
    ones = lax.dynamic_update_slice(ones, sums_one[0:2], (0, y * HALF_D))
    bias = lax.dynamic_update_slice(jnp.zeros((D,), f32), cot_sums[:, 0], (c * col,))
    grad_vector = jnp.concatenate([ones.reshape(-1), grid.reshape(-1), bias, squares[:, 0], jnp.zeros((120,), f32)])
    grad_vector = grad_vector.reshape(-1, 128)
    grad_vector = grad_vector + swap_core(grad_vector)
    grad_vector = grad_vector + swap_y(grad_vector)
    bit = 1
    while bit < S:
        grad_vector = grad_vector + lax.ppermute(grad_vector, "seq", [(i, i ^ bit) for i in range(S)])
        bit *= 2
    grad_vector = grad_vector.reshape(-1)
    total_stats = grad_vector[VECTOR : VECTOR + 3]
    grad_vector = grad_vector[:VECTOR]
    vector_first = adam_first * vector_moment + (1.0 - adam_first) * grad_vector
    vector_second = adam_second * vector_square + (1.0 - adam_second) * grad_vector * grad_vector
    corrected_first = vector_first / (1.0 - adam_first**STEP)
    corrected_second = vector_second / (1.0 - adam_second**STEP)
    vector_values = vector_params - adam_rate * (
        corrected_first / (jnp.sqrt(corrected_second) + adam_eps) + decay_rate * vector_params
    )
    root_means = jnp.sqrt(total_stats[:2] / (total_stats[2] * D))
    return (
        block_output.T,
        tokens_grad.T,
        out_first.T,
        jnp.swapaxes(out_taps, 1, 2),
        out_last,
        new_first.T,
        jnp.swapaxes(new_taps, 1, 2),
        new_last,
        vector_first,
        vector_second,
        vector_values,
        root_means,
    )


def solution(mesh):
    placed = (
        P("seq", None),
        P("seq", "ch"),
        P(),
        P("seq"),
        P(None, "ch"),
        P(None, None, "ch"),
        P("ch", None),
        P(None, "ch"),
        P(None, None, "ch"),
        P("ch", None),
        P(),
        P(),
        P(),
    )
    return jax.shard_map(
        body,
        mesh=mesh,
        in_specs=placed,
        out_specs=(
            P("seq", "ch"),
            P("seq", "ch"),
            P(None, "ch"),
            P(None, None, "ch"),
            P("ch", None),
            P(None, "ch"),
            P(None, None, "ch"),
            P("ch", None),
            P(),
            P(),
            P(),
            P(),
        ),
        check_vma=False,
    )
```

time: 767 us -> 340 us (0.44); the launches traced: 757 us -> 339 us
  waiting for transfers between devices: 400 us -> 146 us
  blocking collectives: 106 us -> 0 us
  Pallas kernels: 0 us -> 97.4 us
  other arithmetic: 76.3 us -> 3.16 us
  starting transfers between devices: 12.3 us -> 56.5 us
  loops' own time: 41.6 us -> 0 us
  local copies, waits for them, and re-layouts: 70.9 us -> 33.5 us
  matrix products: 31.6 us -> 0 us
  between operations: 17.7 us -> 2.12 us
    psum x2 -> x0, waiting for transfers between devices: 193 us -> none  [the longest x1 145 us: body(): lax.psum((grad_first, grad_dilated, grad_last), 'seq')]
    ppermute x4 -> x46, waiting for transfers between devices: 2.95 us -> 146 us  [the longest x7 53.5 us: swap_x(): return lax.ppermute(v, 'seq', xsw)]
    all_gather x6 -> x0, waiting for transfers between devices: 138 us -> none  [the longest x1 59.4 us: body(): lax.all_gather(dilated_momentum, 'ch', axis=2, tiled=True)]
    psum x5 -> x0, blocking collectives: 106 us -> none  [the longest x1 79.9 us: body(): lax.psum((grad_vector, local_stats), ('seq', 'ch'))]
    pallas_call x0 -> x34, Pallas kernels: none -> 97.4 us  [the longest x33 93.3 us: call(): pl.pallas_call(kernel, out_shape=shapes, in_specs=[SMEM] * len(scalars) +...]
    reduce_scatter x2 -> x0, waiting for transfers between devices: 66.3 us -> none  [the longest x1 36.6 us: body(): lax.psum_scatter(partial_out, 'ch', scatter_dimension=1, tiled=True)]
    ppermute x4 -> x46, starting transfers between devices: 11.9 us -> 56.5 us  [the longest x12 18.2 us: swap_y(): return lax.ppermute(v, 'ch', opp)]
    another operation x1 -> x0, loops' own time: 41.6 us -> none  [body(): packed = lax.switch(owner, branches)]
  transfers between devices with their start and end apart: 14 -> 46, of which waited for: 12 -> 25; matrix products, arithmetic and copies ran while one was open for 9% -> 4% of each run, Pallas kernels for 0% -> 25%
where the time goes in v1:
time: 340 us; the launch traced here: 339 us
  waiting for transfers between devices  146 us (43%)
  Pallas kernels  97.4 us (29%)
  starting transfers between devices  56.5 us (17%)
  local copies, waits for them, and re-layouts  33.5 us (10%)
    pallas_call x33, Pallas kernels, call(): pl.pallas_call(kernel, out_shape=shapes, in_specs=[SMEM] * len(scalars) +...  93.3 us
    ppermute x7, waiting for transfers between devices, swap_x(): return lax.ppermute(v, 'seq', xsw)  53.5 us
    ppermute x8, waiting for transfers between devices, along_h(): lax.ppermute(v, 'seq', [(2 * i + q, 2 * j + q) for i, j in pairs for q in...  36.4 us
    ppermute x12, waiting for transfers between devices, swap_y(): return lax.ppermute(v, 'ch', opp)  35 us
    unnamed x125, local copies, waits for them, and re-layouts  23.4 us
    ppermute x12, starting transfers between devices, swap_y(): return lax.ppermute(v, 'ch', opp)  18.2 us
    ppermute x8, starting transfers between devices, along_h(): lax.ppermute(v, 'seq', [(2 * i + q, 2 * j + q) for i, j in pairs for q in...  14.6 us
    ppermute x3, waiting for transfers between devices, body(): lax.ppermute(grad_vector, 'seq', [(i, i ^ bit) for i in range(S)])  14.1 us
  transfers between devices with their start and end apart: 46, of which 25 were waited for; matrix products, arithmetic and copies ran while one was open for 4% of the time, Pallas kernels for 25%

profile of v1, /device:TPU:0, one launch (start us, length us, event | category | flops | bytes accessed | tf_op | source)
XLA Modules:
  0.0 339.0 jit_solution(14576208648702722671)
XLA Ops:
  3.4 1.5 shard_map.220
  8.8 2.5 copy-done.35
  11.3 4.2 %shard_map.221 = (bf16[512,1280]{1,0:T(8,128)(2,1)S(1)}, bf16[512,1280]{1,0:T(8,128)(2,1)S(1)}, bf16[512,1280]{1,0:T(8,128)(2,1)S(1)}, f32[512,128]{1,0:T(8,128)S(1)}) custom-call(s32[6]{0:T(128)S(1)} %stack.27.idx, f32[1024,1280]{1,0:T(8,128)S(1)} %copy-done.35, f32[2,1280]{1,0:T(2,128)S(1)} %slice.66.gs_ref), custom_call_target="tpu_custom_call" | custom-call | flops 5000000000 | bytes 8000000 | tf_op jit(solution)/shard_map/pallas_call | solution.py:816
  15.6 2.6 shard_map.222
  18.2 2.7 collective-permute-start.1
  20.9 1.7 collective-permute-done.1.got_ref.stg_ref
  24.0 2.1 collective-permute-start.2
  26.1 7.1 %collective-permute-done.2.got_ref = bf16[320,512]{1,0:T(8,128)(2,1)S(1)} collective-permute-done((bf16[320,512]{1,0:T(8,128)(2,1)S(1)}, bf16[320,512]{1,0:T(8,128)(2,1)S(1)}, u32[]{:S(2)}, u32[]{:S(2)}) %collective-permute-start.2) | collective-permute-done | bytes 327712 | tf_op jit(solution)/shard_map/ppermute | solution.py:775
  34.5 3.1 collective-permute-start.7
  37.7 1.5 collective-permute-start.8
  39.2 3.0 shard_map.226
  42.3 1.5 collective-permute-start.6
  43.7 4.5 %collective-permute-done.8.opp_ref = bf16[320,512]{1,0:T(8,128)(2,1)S(1)} collective-permute-done((bf16[320,512]{1,0:T(8,128)(2,1)S(1)}, bf16[320,512]{1,0:T(8,128)(2,1)S(1)}, u32[]{:S(2)}, u32[]{:S(2)}) %collective-permute-start.8) | collective-permute-done | bytes 327712 | tf_op jit(solution)/shard_map/ppermute | solution.py:775
  48.2 5.4 %collective-permute-done.9.diag_ref = bf16[320,512]{1,0:T(8,128)(2,1)S(1)} collective-permute-done((bf16[320,512]{1,0:T(8,128)(2,1)S(1)}, bf16[320,512]{1,0:T(8,128)(2,1)S(1)}, u32[]{:S(2)}, u32[]{:S(2)}) %collective-permute-start.9) | collective-permute-done | bytes 327712 | tf_op jit(solution)/shard_map/ppermute | solution.py:812
  56.7 1.5 collective-permute-start.12
  58.2 2.3 collective-permute-done.12.got_ref
  61.9 3.8 %shard_map.241 = (f32[160,4480]{1,0:T(8,128)S(1)}, bf16[160,4480]{1,0:T(8,128)(2,1)}) custom-call(s32[6]{0:T(128)S(1)} %stack.27.idx, bf16[320,512]{1,0:T(8,128)(2,1)S(1)} %get-tuple-element.104.dz_ref, bf16[640,1024]{1,0:T(8,128)(2,1)S(1)} %get-tuple-element.126.ext_ref, f32[8,512]{1,0:T(8,128)S(1)} %get-tuple-element.107.mask_ref, ...), custom_call_target="tpu_custom_call" | custom-call | flops 1600000000 | bytes 7593984 | tf_op jit(solution)/shard_map/pallas_call | solution.py:67
  66.9 1.9 collective-permute-done.13.in_ref
  68.8 2.6 shard_map.233
  71.4 1.6 collective-permute-start.15
  73.0 5.6 %collective-permute-done.15.got_ref = bf16[320,512]{1,0:T(8,128)(2,1)S(1)} collective-permute-done((bf16[320,512]{1,0:T(8,128)(2,1)S(1)}, bf16[320,512]{1,0:T(8,128)(2,1)S(1)}, u32[]{:S(2)}, u32[]{:S(2)}) %collective-permute-start.15) | collective-permute-done | bytes 327712 | tf_op jit(solution)/shard_map/ppermute | solution.py:775
  78.8 1.6 collective-permute-start.16
  80.4 2.3 collective-permute-done.16.got_ref
  82.7 2.2 shard_map.235
  86.5 2.9 collective-permute-start.24
  89.4 1.8 copy-done.17
  91.3 1.9 shard_map.242
  93.1 6.3 %collective-permute-start.21 = (bf16[160,2240]{1,0:T(8,128)(2,1)}, bf16[160,2240]{1,0:T(8,128)(2,1)S(1)}, u32[]{:S(2)}, u32[]{:S(2)}) collective-permute-start(bf16[160,2240]{1,0:T(8,128)(2,1)} %get-tuple-element.131), channel_id=1, source_target_pairs={{0,4},{4,0},{8,12},{12,8},{16,20},{20,16},{24,28},{28,24},{1,5},{5... | collective-permute-start | bytes 2150408 | tf_op jit(solution)/shard_map/ppermute | solution.py:778
  101.5 15.4 %collective-permute-done.21.got_ref = bf16[160,2240]{1,0:T(8,128)(2,1)S(1)} collective-permute-done((bf16[160,2240]{1,0:T(8,128)(2,1)}, bf16[160,2240]{1,0:T(8,128)(2,1)S(1)}, u32[]{:S(2)}, u32[]{:S(2)}) %collective-permute-start.21) | collective-permute-done | bytes 716832 | tf_op jit(solution)/shard_map/ppermute | solution.py:778
  117.7 3.3 collective-permute-start.22
  121.2 5.1 %collective-permute-start.26 = (bf16[160,640]{1,0:T(8,128)(2,1)S(1)}, bf16[160,640]{1,0:T(8,128)(2,1)S(1)}, u32[]{:S(2)}, u32[]{:S(2)}) collective-permute-start(bf16[160,640]{1,0:T(8,128)(2,1)S(1)} %fusion), channel_id=1, source_target_pairs={{0,8},{4,12},{16,24},{20,28},{1,9},{5,13},{17,25},{21,29},{2,10},{... | collective-permute-start | bytes 614408 | tf_op jit(solution)/shard_map/ppermute | solution.py:781
  126.2 4.7 %collective-permute-done.22.got_ref = bf16[160,1280]{1,0:T(8,128)(2,1)S(1)} collective-permute-done((bf16[160,1280]{1,0:T(8,128)(2,1)S(1)}, bf16[160,1280]{1,0:T(8,128)(2,1)S(1)}, u32[]{:S(2)}, u32[]{:S(2)}) %collective-permute-start.22) | collective-permute-done | bytes 409632 | tf_op jit(solution)/shard_map/ppermute | solution.py:781
  131.6 2.7 collective-permute-start.23
  136.6 14.5 %collective-permute-done.23.got_ref = bf16[160,960]{1,0:T(8,128)(2,1)S(1)} collective-permute-done((bf16[160,960]{1,0:T(8,128)(2,1)S(1)}, bf16[160,960]{1,0:T(8,128)(2,1)S(1)}, u32[]{:S(2)}, u32[]{:S(2)}) %collective-permute-start.23) | collective-permute-done | bytes 307232 | tf_op jit(solution)/shard_map/ppermute | solution.py:781
  152.7 5.9 %collective-permute-done.28.got_ref = bf16[160,640]{1,0:T(8,128)(2,1)S(1)} collective-permute-done((bf16[160,640]{1,0:T(8,128)(2,1)S(1)}, bf16[160,640]{1,0:T(8,128)(2,1)S(1)}, u32[]{:S(2)}, u32[]{:S(2)}) %collective-permute-start.28) | collective-permute-done | bytes 204832 | tf_op jit(solution)/shard_map/ppermute | solution.py:778
  160.0 1.5 collective-permute-start.30
  161.5 8.3 %collective-permute-done.30.opp_ref = bf16[160,1280]{1,0:T(8,128)(2,1)} collective-permute-done((bf16[160,1280]{1,0:T(8,128)(2,1)}, bf16[160,1280]{1,0:T(8,128)(2,1)}, u32[]{:S(2)}, u32[]{:S(2)}) %collective-permute-start.30) | collective-permute-done | bytes 409632 | tf_op jit(solution)/shard_map/ppermute | solution.py:775
  173.4 2.4 shard_map.229
  176.9 1.5 collective-permute-start.10
  178.4 2.4 shard_map.236
  182.4 39.9 %shard_map.248 = (bf16[160,1280]{1,0:T(8,128)(2,1)S(1)}, bf16[160,640]{1,0:T(8,128)(2,1)}) custom-call(s32[6]{0:T(128)S(1)} %stack.27.idx, bf16[160,1280]{1,0:T(8,128)(2,1)} %shard_map.247.own_ref, bf16[160,1280]{1,0:T(8,128)(2,1)} %collective-permute-done.29.sib_ref, bf16[160,1280]{1,0:T(8,128)(2,1)} %collective-permute-done.30.opp_ref, ...), custom_call_target="tpu_custom_call" | custom-call | flops 30000001024 | bytes 2252800 | tf_op jit(solution)/shard_map/pallas_call | solution.py:67
  223.8 1.4 dynamic_update_slice.11
  226.0 1.6 copy.30
  232.8 3.4 %shard_map.230 = (f32[320,512]{1,0:T(8,128)S(1)}, f32[320,512]{1,0:T(8,128)}, f32[8,128]{1,0:T(8,128)S(1)}) custom-call(s32[6]{0:T(128)S(1)} %stack.27.idx, f32[512,640]{1,0:T(8,128)S(1)} %copy-done.19, bf16[512,640]{1,0:T(8,128)(2,1)} %collective-permute-done.10.got_ref, f32[512,640]{1,0:T(8,128)S(1)} %dynamic_slice.13.tok_ref, ...), custom_call_target="tpu_custom_call" | custom-call | flops 100000000 | bytes 4600832 | tf_op jit(solution)/shard_map/pallas_call | solution.py:67
  237.5 1.7 shard_map.249.own_ref
  239.2 2.7 collective-permute-start.33
  242.1 1.8 shard_map.237
  245.3 11.5 %collective-permute-done.37.got_ref = bf16[160,960]{1,0:T(8,128)(2,1)} collective-permute-done((bf16[160,960]{1,0:T(8,128)(2,1)}, bf16[160,960]{1,0:T(8,128)(2,1)}, u32[]{:S(2)}, u32[]{:S(2)}) %collective-permute-start.37) | collective-permute-done | bytes 307232 | tf_op jit(solution)/shard_map/ppermute | solution.py:781
  259.2 4.8 %collective-permute-done.33.got_ref = bf16[160,960]{1,0:T(8,128)(2,1)} collective-permute-done((bf16[160,960]{1,0:T(8,128)(2,1)}, bf16[160,960]{1,0:T(8,128)(2,1)}, u32[]{:S(2)}, u32[]{:S(2)}) %collective-permute-start.33) | collective-permute-done | bytes 307232 | tf_op jit(solution)/shard_map/ppermute | solution.py:781
  265.2 1.6 collective-permute-start.42
  267.4 3.3 collective-permute-done.18.got_ref
  270.7 1.4 shard_map.239
  273.2 3.0 collective-permute-done.43
  276.2 2.0 collective-permute-start.44
  278.3 8.9 %collective-permute-done.44 = f32[61,128]{1,0:T(8,128)S(1)} collective-permute-done((f32[61,128]{1,0:T(8,128)S(1)}, f32[61,128]{1,0:T(8,128)S(1)}, u32[]{:S(2)}, u32[]{:S(2)}) %collective-permute-start.44) | collective-permute-done | bytes 31264 | tf_op jit(solution)/shard_map/ppermute | solution.py:1085
  290.0 2.2 collective-permute-done.45
  294.2 2.3 shard_map.231
  299.0 1.7 shard_map.240
  300.7 2.2 collective-permute-done.38.x_ref
  303.0 11.4 %collective-permute-done.40.zx_ref = bf16[160,1600]{1,0:T(8,128)(2,1)S(1)} collective-permute-done((bf16[160,1600]{1,0:T(8,128)(2,1)S(1)}, bf16[160,1600]{1,0:T(8,128)(2,1)S(1)}, u32[]{:S(2)}, u32[]{:S(2)}) %collective-permute-start.40) | collective-permute-done | bytes 512032 | tf_op jit(solution)/shard_map/ppermute | solution.py:778
  314.4 3.1 shard_map.253
  317.5 8.3 %collective-permute-done.34.x_ref = bf16[160,1600]{1,0:T(8,128)(2,1)S(1)} collective-permute-done((bf16[160,1600]{1,0:T(8,128)(2,1)S(1)}, bf16[160,1600]{1,0:T(8,128)(2,1)S(1)}, u32[]{:S(2)}, u32[]{:S(2)}) %collective-permute-start.34) | collective-permute-done | bytes 512032 | tf_op jit(solution)/shard_map/ppermute | solution.py:778
  325.8 10.1 %collective-permute-done.36.zx_ref = bf16[160,1600]{1,0:T(8,128)(2,1)S(1)} collective-permute-done((bf16[160,1600]{1,0:T(8,128)(2,1)S(1)}, bf16[160,1600]{1,0:T(8,128)(2,1)S(1)}, u32[]{:S(2)}, u32[]{:S(2)}) %collective-permute-start.36) | collective-permute-done | bytes 512032 | tf_op jit(solution)/shard_map/ppermute | solution.py:778
  336.0 3.0 shard_map.251
  (228 shorter events, 54.1 us)
Async XLA Ops:
  6.2 9.3 %collective-permute-start = (bf16[160,1280]{1,0:T(8,128)(2,1)}, bf16[160,1280]{1,0:T(8,128)(2,1)}, u32[]{:S(2)}, u32[]{:S(2)}) collective-permute-start(bf16[160,1280]{1,0:T(8,128)(2,1)} %get-tuple-element.83.own_ref), channel_id=1, source_target_pairs={{0,1},{1,0},{2,3},{3,2},{4,5},{5,4},{6,7},{7,6},{8,9},{9,8},{10,11... | collective-permute-start | bytes 1228808 | tf_op jit(solution)/shard_map/ppermute | solution.py:772
  8.0 31.2 %collective-permute-start.5 = (bf16[160,4480]{1,0:T(8,128)(2,1)S(1)}, bf16[160,4480]{1,0:T(8,128)(2,1)}, u32[]{:S(2)}, u32[]{:S(2)}) collective-permute-start(bf16[160,4480]{1,0:T(8,128)(2,1)S(1)} %shard_map.225.wo_ref), channel_id=1, source_target_pairs={{0,1},{1,0},{2,3},{3,2},{4,5},{5,4},{6,7},{7,6},{8,9},{9,8},{10,11... | collective-permute-start | bytes 4300808 | tf_op jit(solution)/shard_map/ppermute | solution.py:772
  15.5 19.0 %copy-start.51 = (bf16[320,512]{1,0:T(8,128)(2,1)S(1)}, bf16[320,512]{1,0:T(8,128)(2,1)}, u32[]{:S(2)}) copy-start(bf16[320,512]{1,0:T(8,128)(2,1)} %copy-done.50) | copy-start | bytes 983044
  15.5 22.1 %copy-start.34 = (bf16[320,512]{1,0:T(8,128)(2,1)S(1)}, bf16[320,512]{1,0:T(8,128)(2,1)}, u32[]{:S(2)}) copy-start(bf16[320,512]{1,0:T(8,128)(2,1)} %copy-done.33) | copy-start | bytes 983044
  15.6 23.6 %copy-start.43 = (s32[16]{0:T(128)S(1)}, s32[16]{0:T(128)}, u32[]{:S(2)}) copy-start(s32[16]{0:T(128)} %lengths.1) | copy-start | bytes 196
  18.2 15.7 %copy-start.44 = (bf16[320,1280]{1,0:T(8,128)(2,1)}, bf16[320,1280]{1,0:T(8,128)(2,1)S(1)}, u32[]{:S(2)}) copy-start(bf16[320,1280]{1,0:T(8,128)(2,1)S(1)} %get-tuple-element.116.w_ref) | copy-start | bytes 2457604
  18.2 4.4 %collective-permute-start.1 = (f32[8,512]{1,0:T(8,128)S(1)}, f32[8,512]{1,0:T(8,128)S(1)}, u32[]{:S(2)}, u32[]{:S(2)}) collective-permute-start(f32[8,512]{1,0:T(8,128)S(1)} %get-tuple-element.86.st_ref), channel_id=1, source_target_pairs={{0,2},{1,3},{2,0},{3,1},{4,6},{5,7},{6,4},{7,5},{8,10},{9,11},{10,... | collective-permute-start | bytes 49160 | tf_op jit(solution)/shard_map/ppermute | solution.py:775
  24.0 9.2 %collective-permute-start.2 = (bf16[320,512]{1,0:T(8,128)(2,1)S(1)}, bf16[320,512]{1,0:T(8,128)(2,1)S(1)}, u32[]{:S(2)}, u32[]{:S(2)}) collective-permute-start(bf16[320,512]{1,0:T(8,128)(2,1)S(1)} %get-tuple-element.87.own_ref), channel_id=1, source_target_pairs={{0,2},{1,3},{2,0},{3,1},{4,6},{5,7},{6,4},{7,5},{8,10},{9,11},{10,... | collective-permute-start | bytes 983048 | tf_op jit(solution)/shard_map/ppermute | solution.py:775
  33.8 5.4 %collective-permute-start.3 = (bf16[640,256]{1,0:T(8,128)(2,1)S(1)}, bf16[640,256]{1,0:T(8,128)(2,1)S(1)}, u32[]{:S(2)}, u32[]{:S(2)}) collective-permute-start(bf16[640,256]{1,0:T(8,128)(2,1)S(1)} %get-tuple-element.88), channel_id=1, source_target_pairs={{0,1},{1,0},{2,3},{3,2},{4,5},{5,4},{6,7},{7,6},{8,9},{9,8},{10,11... | collective-permute-start | bytes 983048 | tf_op jit(solution)/shard_map/ppermute | solution.py:772
  33.8 5.3 %collective-permute-start.4 = (bf16[640,256]{1,0:T(8,128)(2,1)S(1)}, bf16[640,256]{1,0:T(8,128)(2,1)S(1)}, u32[]{:S(2)}, u32[]{:S(2)}) collective-permute-start(bf16[640,256]{1,0:T(8,128)(2,1)S(1)} %get-tuple-element.89), channel_id=1, source_target_pairs={{1,4},{3,6},{4,1},{5,8},{6,3},{7,10},{8,5},{9,12},{10,7},{11,14},{... | collective-permute-start | bytes 983048 | tf_op jit(solution)/shard_map/ppermute | solution.py:792
  34.5 9.2 %collective-permute-start.7 = (bf16[320,512]{1,0:T(8,128)(2,1)S(1)}, bf16[320,512]{1,0:T(8,128)(2,1)S(1)}, u32[]{:S(2)}, u32[]{:S(2)}) collective-permute-start(bf16[320,512]{1,0:T(8,128)(2,1)S(1)} %copy-done.51), channel_id=1, source_target_pairs={{0,1},{1,0},{2,3},{3,2},{4,5},{5,4},{6,7},{7,6},{8,9},{9,8},{10,11... | collective-permute-start | bytes 983048 | tf_op jit(solution)/shard_map/ppermute | solution.py:772
  37.7 10.6 %collective-permute-start.8 = (bf16[320,512]{1,0:T(8,128)(2,1)S(1)}, bf16[320,512]{1,0:T(8,128)(2,1)S(1)}, u32[]{:S(2)}, u32[]{:S(2)}) collective-permute-start(bf16[320,512]{1,0:T(8,128)(2,1)S(1)} %copy-done.34), channel_id=1, source_target_pairs={{0,2},{1,3},{2,0},{3,1},{4,6},{5,7},{6,4},{7,5},{8,10},{9,11},{10,... | collective-permute-start | bytes 983048 | tf_op jit(solution)/shard_map/ppermute | solution.py:775
  39.2 14.4 %collective-permute-start.9 = (bf16[320,512]{1,0:T(8,128)(2,1)S(1)}, bf16[320,512]{1,0:T(8,128)(2,1)S(1)}, u32[]{:S(2)}, u32[]{:S(2)}) collective-permute-start(bf16[320,512]{1,0:T(8,128)(2,1)S(1)} %copy-done.51), channel_id=1, source_target_pairs={{0,3},{1,2},{2,1},{3,0},{4,7},{5,6},{6,5},{7,4},{8,11},{9,10},{10,... | collective-permute-start | bytes 983048 | tf_op jit(solution)/shard_map/ppermute | solution.py:812
  42.3 13.5 %collective-permute-start.6 = (f32[8,512]{1,0:T(8,128)S(1)}, f32[8,512]{1,0:T(8,128)S(1)}, u32[]{:S(2)}, u32[]{:S(2)}) collective-permute-start(f32[8,512]{1,0:T(8,128)S(1)} %get-tuple-element.91.st_ref), channel_id=1, source_target_pairs={{0,2},{1,3},{2,0},{3,1},{4,6},{5,7},{6,4},{7,5},{8,10},{9,11},{10,... | collective-permute-start | bytes 49160 | tf_op jit(solution)/shard_map/ppermute | solution.py:775
  56.7 3.8 %collective-permute-start.12 = (f32[8,512]{1,0:T(8,128)S(1)}, f32[8,512]{1,0:T(8,128)S(1)}, u32[]{:S(2)}, u32[]{:S(2)}) collective-permute-start(f32[8,512]{1,0:T(8,128)S(1)} %get-tuple-element.103.part_ref), channel_id=1, source_target_pairs={{0,2},{1,3},{2,0},{3,1},{4,6},{5,7},{6,4},{7,5},{8,10},{9,11},{10,... | collective-permute-start | bytes 49160 | tf_op jit(solution)/shard_map/ppermute | solution.py:775
  65.7 23.7 %collective-permute-start.20 = (bf16[160,4480]{1,0:T(8,128)(2,1)}, bf16[160,4480]{1,0:T(8,128)(2,1)S(1)}, u32[]{:S(2)}, u32[]{:S(2)}) collective-permute-start(bf16[160,4480]{1,0:T(8,128)(2,1)} %get-tuple-element.129), channel_id=1, source_target_pairs={{0,1},{1,0},{2,3},{3,2},{4,5},{5,4},{6,7},{7,6},{8,9},{9,8},{10,11... | collective-permute-start | bytes 4300808 | tf_op jit(solution)/shard_map/ppermute | solution.py:772
  65.7 3.1 collective-permute-start.13
  66.2 2.6 collective-permute-start.14
  71.4 7.1 %collective-permute-start.15 = (bf16[320,512]{1,0:T(8,128)(2,1)S(1)}, bf16[320,512]{1,0:T(8,128)(2,1)S(1)}, u32[]{:S(2)}, u32[]{:S(2)}) collective-permute-start(bf16[320,512]{1,0:T(8,128)(2,1)S(1)} %get-tuple-element.110), channel_id=1, source_target_pairs={{0,2},{1,3},{2,0},{3,1},{4,6},{5,7},{6,4},{7,5},{8,10},{9,11},{10,... | collective-permute-start | bytes 983048 | tf_op jit(solution)/shard_map/ppermute | solution.py:775
  78.8 3.9 %collective-permute-start.16 = (f32[8,512]{1,0:T(8,128)S(1)}, f32[8,512]{1,0:T(8,128)S(1)}, u32[]{:S(2)}, u32[]{:S(2)}) collective-permute-start(f32[8,512]{1,0:T(8,128)S(1)} %get-tuple-element.114.part_ref), channel_id=1, source_target_pairs={{0,2},{1,3},{2,0},{3,1},{4,6},{5,7},{6,4},{7,5},{8,10},{9,11},{10,... | collective-permute-start | bytes 49160 | tf_op jit(solution)/shard_map/ppermute | solution.py:775
  86.5 31.2 %copy-start.28 = (f32[320,8]{1,0:T(8,128)}, f32[320,8]{1,0:T(8,128)S(1)}, u32[]{:S(2)}) copy-start(f32[320,8]{1,0:T(8,128)S(1)} %get-tuple-element.150) | copy-start | bytes 30724
  86.5 12.9 %collective-permute-start.24 = (bf16[160,1280]{1,0:T(8,128)(2,1)}, bf16[160,1280]{1,0:T(8,128)(2,1)}, u32[]{:S(2)}, u32[]{:S(2)}) collective-permute-start(bf16[160,1280]{1,0:T(8,128)(2,1)} %get-tuple-element.137), channel_id=1, source_target_pairs={{0,1},{1,0},{2,3},{3,2},{4,5},{5,4},{6,7},{7,6},{8,9},{9,8},{10,11... | collective-permute-start | bytes 1228808 | tf_op jit(solution)/shard_map/ppermute | solution.py:772
  93.1 23.8 %collective-permute-start.21 = (bf16[160,2240]{1,0:T(8,128)(2,1)}, bf16[160,2240]{1,0:T(8,128)(2,1)S(1)}, u32[]{:S(2)}, u32[]{:S(2)}) collective-permute-start(bf16[160,2240]{1,0:T(8,128)(2,1)} %get-tuple-element.131), channel_id=1, source_target_pairs={{0,4},{4,0},{8,12},{12,8},{16,20},{20,16},{24,28},{28,24},{1,5},{5... | collective-permute-start | bytes 2150408 | tf_op jit(solution)/shard_map/ppermute | solution.py:778
  101.4 19.7 %collective-permute-start.25 = (bf16[160,640]{1,0:T(8,128)(2,1)S(1)}, bf16[160,640]{1,0:T(8,128)(2,1)S(1)}, u32[]{:S(2)}, u32[]{:S(2)}) collective-permute-start(bf16[160,640]{1,0:T(8,128)(2,1)S(1)} %dynamic-slice_convert_fusion), channel_id=1, source_target_pairs={{0,4},{4,0},{8,12},{12,8},{16,20},{20,16},{24,28},{28,24},{1,5},{5... | collective-permute-start | bytes 614408 | tf_op jit(solution)/shard_map/ppermute | solution.py:778
  101.5 19.6 %copy-start.55 = (f32[160,1280]{1,0:T(8,128)S(1)}, f32[160,1280]{1,0:T(8,128)}, u32[]{:S(2)}) copy-start(f32[160,1280]{1,0:T(8,128)} %copy-done.54) | copy-start | bytes 2457604
  117.7 13.2 %collective-permute-start.22 = (bf16[160,1280]{1,0:T(8,128)(2,1)S(1)}, bf16[160,1280]{1,0:T(8,128)(2,1)S(1)}, u32[]{:S(2)}, u32[]{:S(2)}) collective-permute-start(bf16[160,1280]{1,0:T(8,128)(2,1)S(1)} %get-tuple-element.133), channel_id=1, source_target_pairs={{0,8},{4,12},{8,0},{12,4},{16,24},{20,28},{24,16},{28,20},{1,9},{5... | collective-permute-start | bytes 1228808 | tf_op jit(solution)/shard_map/ppermute | solution.py:781
  121.2 14.0 %collective-permute-start.26 = (bf16[160,640]{1,0:T(8,128)(2,1)S(1)}, bf16[160,640]{1,0:T(8,128)(2,1)S(1)}, u32[]{:S(2)}, u32[]{:S(2)}) collective-permute-start(bf16[160,640]{1,0:T(8,128)(2,1)S(1)} %fusion), channel_id=1, source_target_pairs={{0,8},{4,12},{16,24},{20,28},{1,9},{5,13},{17,25},{21,29},{2,10},{... | collective-permute-start | bytes 614408 | tf_op jit(solution)/shard_map/ppermute | solution.py:781
  131.6 19.5 %collective-permute-start.23 = (bf16[160,960]{1,0:T(8,128)(2,1)S(1)}, bf16[160,960]{1,0:T(8,128)(2,1)S(1)}, u32[]{:S(2)}, u32[]{:S(2)}) collective-permute-start(bf16[160,960]{1,0:T(8,128)(2,1)S(1)} %get-tuple-element.135), channel_id=1, source_target_pairs={{0,16},{4,20},{8,24},{12,28},{16,0},{20,4},{24,8},{28,12},{1,17},{... | collective-permute-start | bytes 921608 | tf_op jit(solution)/shard_map/ppermute | solution.py:781
  135.2 1.3 collective-permute-start.27
  151.1 18.8 %copy-start.57 = (f32[7680]{0:T(1024)S(1)}, f32[7680]{0:T(1024)}, u32[]{:S(2)}) copy-start(f32[7680]{0:T(1024)} %param.23) | copy-start | bytes 92164
  152.5 6.1 %collective-permute-start.28 = (bf16[160,640]{1,0:T(8,128)(2,1)S(1)}, bf16[160,640]{1,0:T(8,128)(2,1)S(1)}, u32[]{:S(2)}, u32[]{:S(2)}) collective-permute-start(bf16[160,640]{1,0:T(8,128)(2,1)S(1)} %get-tuple-element.139), channel_id=1, source_target_pairs={{0,4},{4,0},{8,12},{12,8},{16,20},{20,16},{24,28},{28,24},{1,5},{5... | collective-permute-start | bytes 614408 | tf_op jit(solution)/shard_map/ppermute | solution.py:778
  160.0 9.8 %collective-permute-start.30 = (bf16[160,1280]{1,0:T(8,128)(2,1)}, bf16[160,1280]{1,0:T(8,128)(2,1)}, u32[]{:S(2)}, u32[]{:S(2)}) collective-permute-start(bf16[160,1280]{1,0:T(8,128)(2,1)} %shard_map.247.own_ref), channel_id=1, source_target_pairs={{0,2},{1,3},{2,0},{3,1},{4,6},{5,7},{6,4},{7,5},{8,10},{9,11},{10,... | collective-permute-start | bytes 1228808 | tf_op jit(solution)/shard_map/ppermute | solution.py:775
  161.5 20.9 %collective-permute-start.29 = (bf16[160,1280]{1,0:T(8,128)(2,1)}, bf16[160,1280]{1,0:T(8,128)(2,1)}, u32[]{:S(2)}, u32[]{:S(2)}) collective-permute-start(bf16[160,1280]{1,0:T(8,128)(2,1)} %shard_map.247.own_ref), channel_id=1, source_target_pairs={{0,1},{1,0},{2,3},{3,2},{4,5},{5,4},{6,7},{7,6},{8,9},{9,8},{10,11... | collective-permute-start | bytes 1228808 | tf_op jit(solution)/shard_map/ppermute | solution.py:772
  169.8 12.6 %collective-permute-start.31 = (bf16[160,1280]{1,0:T(8,128)(2,1)}, bf16[160,1280]{1,0:T(8,128)(2,1)}, u32[]{:S(2)}, u32[]{:S(2)}) collective-permute-start(bf16[160,1280]{1,0:T(8,128)(2,1)} %collective-permute-done.30.opp_ref), channel_id=1, source_target_pairs={{0,1},{1,0},{2,3},{3,2},{4,5},{5,4},{6,7},{7,6},{8,9},{9,8},{10,11... | collective-permute-start | bytes 1228808 | tf_op jit(solution)/shard_map/ppermute | solution.py:772
  176.9 54.6 %collective-permute-start.10 = (bf16[512,640]{1,0:T(8,128)(2,1)}, bf16[512,640]{1,0:T(8,128)(2,1)}, u32[]{:S(2)}, u32[]{:S(2)}) collective-permute-start(bf16[512,640]{1,0:T(8,128)(2,1)} %get-tuple-element.98), channel_id=1, source_target_pairs={{0,2},{1,3},{2,0},{3,1},{4,6},{5,7},{6,4},{7,5},{8,10},{9,11},{10,... | collective-permute-start | bytes 1966088 | tf_op jit(solution)/shard_map/ppermute | solution.py:775
  181.9 41.2 %copy-start.41 = (f32[320,128]{1,0:T(8,128)S(1)}, f32[320,128]{1,0:T(8,128)}, u32[]{:S(2)}) copy-start(f32[320,128]{1,0:T(8,128)} %copy-done.40) | copy-start | bytes 491524
  181.9 60.2 %collective-permute-start.17 = (bf16[512,640]{1,0:T(8,128)(2,1)}, bf16[512,640]{1,0:T(8,128)(2,1)}, u32[]{:S(2)}, u32[]{:S(2)}) collective-permute-start(bf16[512,640]{1,0:T(8,128)(2,1)} %get-tuple-element.118), channel_id=1, source_target_pairs={{0,2},{1,3},{2,0},{3,1},{4,6},{5,7},{6,4},{7,5},{8,10},{9,11},{10,... | collective-permute-start | bytes 1966088 | tf_op jit(solution)/shard_map/ppermute | solution.py:775
  223.0 13.2 %collective-permute-start.32 = (bf16[160,640]{1,0:T(8,128)(2,1)}, bf16[160,640]{1,0:T(8,128)(2,1)}, u32[]{:S(2)}, u32[]{:S(2)}) collective-permute-start(bf16[160,640]{1,0:T(8,128)(2,1)} %get-tuple-element.141), channel_id=1, source_target_pairs={{0,1},{1,0},{2,3},{3,2},{4,5},{5,4},{6,7},{7,6},{8,9},{9,8},{10,11... | collective-permute-start | bytes 614408 | tf_op jit(solution)/shard_map/ppermute | solution.py:772
  236.2 20.6 %collective-permute-start.37 = (bf16[160,960]{1,0:T(8,128)(2,1)}, bf16[160,960]{1,0:T(8,128)(2,1)}, u32[]{:S(2)}, u32[]{:S(2)}) collective-permute-start(bf16[160,960]{1,0:T(8,128)(2,1)} %copy-done.36), channel_id=1, source_target_pairs={{0,16},{4,20},{8,24},{12,28},{16,0},{20,4},{24,8},{28,12},{1,17},{... | collective-permute-start | bytes 921608 | tf_op jit(solution)/shard_map/ppermute | solution.py:781
  239.2 24.7 %collective-permute-start.33 = (bf16[160,960]{1,0:T(8,128)(2,1)}, bf16[160,960]{1,0:T(8,128)(2,1)}, u32[]{:S(2)}, u32[]{:S(2)}) collective-permute-start(bf16[160,960]{1,0:T(8,128)(2,1)} %shard_map.249.own_ref), channel_id=1, source_target_pairs={{0,16},{4,20},{8,24},{12,28},{16,0},{20,4},{24,8},{28,12},{1,17},{... | collective-permute-start | bytes 921608 | tf_op jit(solution)/shard_map/ppermute | solution.py:781
  242.0 46.0 %collective-permute-start.11 = (f32[320,512]{1,0:T(8,128)}, f32[320,512]{1,0:T(8,128)}, u32[]{:S(2)}, u32[]{:S(2)}) collective-permute-start(f32[320,512]{1,0:T(8,128)} %get-tuple-element.100), channel_id=1, source_target_pairs={{0,1},{1,0},{2,3},{3,2},{4,5},{5,4},{6,7},{7,6},{8,9},{9,8},{10,11... | collective-permute-start | bytes 1966088 | tf_op jit(solution)/shard_map/ppermute | solution.py:772
  244.8 25.9 %copy-start.7 = (bf16[512,1280]{1,0:T(8,128)(2,1)S(1)}, bf16[512,1280]{1,0:T(8,128)(2,1)}, u32[]{:S(2)}) copy-start(bf16[512,1280]{1,0:T(8,128)(2,1)} %copy-done.5) | copy-start | bytes 3932164
  244.8 20.3 %collective-permute-start.41 = (f32[61,128]{1,0:T(8,128)S(1)}, f32[61,128]{1,0:T(8,128)S(1)}, u32[]{:S(2)}, u32[]{:S(2)}) collective-permute-start(f32[61,128]{1,0:T(8,128)S(1)} %bitcast.60), channel_id=1, source_target_pairs={{0,1},{1,0},{2,3},{3,2},{4,5},{5,4},{6,7},{7,6},{8,9},{9,8},{10,11... | collective-permute-start | bytes 93704 | tf_op jit(solution)/shard_map/ppermute | solution.py:772
  258.9 30.0 %collective-permute-start.39 = (bf16[160,1600]{1,0:T(8,128)(2,1)S(1)}, bf16[160,1600]{1,0:T(8,128)(2,1)S(1)}, u32[]{:S(2)}, u32[]{:S(2)}) collective-permute-start(bf16[160,1600]{1,0:T(8,128)(2,1)S(1)} %shard_map.252.own_ref), channel_id=1, source_target_pairs={{0,8},{4,12},{8,0},{12,4},{16,24},{20,28},{24,16},{28,20},{1,9},{5... | collective-permute-start | bytes 1536008 | tf_op jit(solution)/shard_map/ppermute | solution.py:781
  265.1 28.0 %collective-permute-start.35 = (bf16[160,1600]{1,0:T(8,128)(2,1)S(1)}, bf16[160,1600]{1,0:T(8,128)(2,1)S(1)}, u32[]{:S(2)}, u32[]{:S(2)}) collective-permute-start(bf16[160,1600]{1,0:T(8,128)(2,1)S(1)} %shard_map.250.own_ref), channel_id=1, source_target_pairs={{0,8},{4,12},{8,0},{12,4},{16,24},{20,28},{24,16},{28,20},{1,9},{5... | collective-permute-start | bytes 1536008 | tf_op jit(solution)/shard_map/ppermute | solution.py:781
  265.2 7.0 %collective-permute-start.42 = (f32[61,128]{1,0:T(8,128)S(1)}, f32[61,128]{1,0:T(8,128)S(1)}, u32[]{:S(2)}, u32[]{:S(2)}) collective-permute-start(f32[61,128]{1,0:T(8,128)S(1)} %bitcast_add_fusion), channel_id=1, source_target_pairs={{0,2},{1,3},{2,0},{3,1},{4,6},{5,7},{6,4},{7,5},{8,10},{9,11},{10,... | collective-permute-start | bytes 93704 | tf_op jit(solution)/shard_map/ppermute | solution.py:775
  266.9 3.8 %collective-permute-start.18 = (f32[8,512]{1,0:T(8,128)S(1)}, f32[8,512]{1,0:T(8,128)S(1)}, u32[]{:S(2)}, u32[]{:S(2)}) collective-permute-start(f32[8,512]{1,0:T(8,128)S(1)} %shard_map.238.part_ref), channel_id=1, source_target_pairs={{0,2},{1,3},{2,0},{3,1},{4,6},{5,7},{6,4},{7,5},{8,10},{9,11},{10,... | collective-permute-start | bytes 49160 | tf_op jit(solution)/shard_map/ppermute | solution.py:775
  270.7 23.5 %copy-start.30 = (f32[320,512]{1,0:T(8,128)S(1)}, f32[320,512]{1,0:T(8,128)}, u32[]{:S(2)}) copy-start(f32[320,512]{1,0:T(8,128)} %copy-done.29) | copy-start | bytes 1966084
  272.1 26.9 %collective-permute-start.19 = (f32[320,512]{1,0:T(8,128)S(1)}, f32[320,512]{1,0:T(8,128)S(1)}, u32[]{:S(2)}, u32[]{:S(2)}) collective-permute-start(f32[320,512]{1,0:T(8,128)S(1)} %get-tuple-element.125), channel_id=1, source_target_pairs={{0,1},{1,0},{2,3},{3,2},{4,5},{5,4},{6,7},{7,6},{8,9},{9,8},{10,11... | collective-permute-start | bytes 1966088 | tf_op jit(solution)/shard_map/ppermute | solution.py:772
  272.2 4.0 %collective-permute-start.43 = (f32[61,128]{1,0:T(8,128)S(1)}, f32[61,128]{1,0:T(8,128)S(1)}, u32[]{:S(2)}, u32[]{:S(2)}) collective-permute-start(f32[61,128]{1,0:T(8,128)S(1)} %fusion.5), channel_id=1, source_target_pairs={{0,4},{4,0},{8,12},{12,8},{16,20},{20,16},{24,28},{28,24},{1,5},{5... | collective-permute-start | bytes 93704 | tf_op jit(solution)/shard_map/ppermute | solution.py:1085
  276.2 22.1 %copy-start.58 = (f32[7680]{0:T(1024)S(1)}, f32[7680]{0:T(1024)}, u32[]{:S(2)}) copy-start(f32[7680]{0:T(1024)} %param.23) | copy-start | bytes 92164
  276.2 22.1 %copy-start.59 = (f32[7680]{0:T(1024)S(1)}, f32[7680]{0:T(1024)}, u32[]{:S(2)}) copy-start(f32[7680]{0:T(1024)} %param.25) | copy-start | bytes 92164
  276.2 22.1 %copy-start.60 = (f32[7680]{0:T(1024)S(1)}, f32[7680]{0:T(1024)}, u32[]{:S(2)}) copy-start(f32[7680]{0:T(1024)} %param.24) | copy-start | bytes 92164
  276.2 11.0 %collective-permute-start.44 = (f32[61,128]{1,0:T(8,128)S(1)}, f32[61,128]{1,0:T(8,128)S(1)}, u32[]{:S(2)}, u32[]{:S(2)}) collective-permute-start(f32[61,128]{1,0:T(8,128)S(1)} %add.85), channel_id=1, source_target_pairs={{0,8},{4,12},{8,0},{12,4},{16,24},{20,28},{24,16},{28,20},{1,9},{5... | collective-permute-start | bytes 93704 | tf_op jit(solution)/shard_map/ppermute | solution.py:1085
  287.2 4.9 %collective-permute-start.45 = (f32[61,128]{1,0:T(8,128)S(1)}, f32[61,128]{1,0:T(8,128)S(1)}, u32[]{:S(2)}, u32[]{:S(2)}) collective-permute-start(f32[61,128]{1,0:T(8,128)S(1)} %add.86), channel_id=1, source_target_pairs={{0,16},{4,20},{8,24},{12,28},{16,0},{20,4},{24,8},{28,12},{1,17},{... | collective-permute-start | bytes 93704 | tf_op jit(solution)/shard_map/ppermute | solution.py:1085
  288.0 15.0 %collective-permute-start.38 = (bf16[160,1600]{1,0:T(8,128)(2,1)S(1)}, bf16[160,1600]{1,0:T(8,128)(2,1)S(1)}, u32[]{:S(2)}, u32[]{:S(2)}) collective-permute-start(bf16[160,1600]{1,0:T(8,128)(2,1)S(1)} %shard_map.252.own_ref), channel_id=1, source_target_pairs={{0,4},{4,0},{8,12},{12,8},{16,20},{20,16},{24,28},{28,24},{1,5},{5... | collective-permute-start | bytes 1536008 | tf_op jit(solution)/shard_map/ppermute | solution.py:778
  288.9 25.5 %collective-permute-start.40 = (bf16[160,1600]{1,0:T(8,128)(2,1)S(1)}, bf16[160,1600]{1,0:T(8,128)(2,1)S(1)}, u32[]{:S(2)}, u32[]{:S(2)}) collective-permute-start(bf16[160,1600]{1,0:T(8,128)(2,1)S(1)} %collective-permute-done.39.z_ref), channel_id=1, source_target_pairs={{0,4},{4,0},{8,12},{12,8},{16,20},{20,16},{24,28},{28,24},{1,5},{5... | collective-permute-start | bytes 1536008 | tf_op jit(solution)/shard_map/ppermute | solution.py:778
  292.2 33.6 %collective-permute-start.34 = (bf16[160,1600]{1,0:T(8,128)(2,1)S(1)}, bf16[160,1600]{1,0:T(8,128)(2,1)S(1)}, u32[]{:S(2)}, u32[]{:S(2)}) collective-permute-start(bf16[160,1600]{1,0:T(8,128)(2,1)S(1)} %shard_map.250.own_ref), channel_id=1, source_target_pairs={{0,4},{4,0},{8,12},{12,8},{16,20},{20,16},{24,28},{28,24},{1,5},{5... | collective-permute-start | bytes 1536008 | tf_op jit(solution)/shard_map/ppermute | solution.py:778
  293.1 42.8 %collective-permute-start.36 = (bf16[160,1600]{1,0:T(8,128)(2,1)S(1)}, bf16[160,1600]{1,0:T(8,128)(2,1)S(1)}, u32[]{:S(2)}, u32[]{:S(2)}) collective-permute-start(bf16[160,1600]{1,0:T(8,128)(2,1)S(1)} %collective-permute-done.35.z_ref), channel_id=1, source_target_pairs={{0,4},{4,0},{8,12},{12,8},{16,20},{20,16},{24,28},{28,24},{1,5},{5... | collective-permute-start | bytes 1536008 | tf_op jit(solution)/shard_map/ppermute | solution.py:778
  299.0 15.4 %copy-start.9 = (f32[1280,160]{0,1:T(8,128)S(1)}, f32[1280,160]{0,1:T(8,128)}, u32[]{:S(2)}) copy-start(f32[1280,160]{0,1:T(8,128)} %param.20) | copy-start | bytes 2457604
  299.0 15.4 %copy-start.11 = (f32[160,1280]{1,0:T(8,128)S(1)}, f32[160,1280]{1,0:T(8,128)}, u32[]{:S(2)}) copy-start(f32[160,1280]{1,0:T(8,128)} %last_ref.7) | copy-start | bytes 2457604
  300.7 35.2 %copy-start.2 = (f32[5,640,160]{1,2,0:T(8,128)S(1)}, f32[5,640,160]{1,2,0:T(8,128)}, u32[]{:S(2)}) copy-start(f32[5,640,160]{1,2,0:T(8,128)} %param.18) | copy-start | bytes 6144004
  300.7 35.2 %copy-start.13 = (f32[1280,160]{0,1:T(8,128)S(1)}, f32[1280,160]{0,1:T(8,128)}, u32[]{:S(2)}) copy-start(f32[1280,160]{0,1:T(8,128)} %param.17) | copy-start | bytes 2457604
  300.7 35.2 %copy-start.15 = (f32[160,1280]{1,0:T(8,128)S(1)}, f32[160,1280]{1,0:T(8,128)}, u32[]{:S(2)}) copy-start(f32[160,1280]{1,0:T(8,128)} %last_ref.6) | copy-start | bytes 2457604
  (45 other events, 187.2 us)
